TPU v7x, 128 devices: a whole 4x4x4 slice. The times are simulated.
128 devices in a mesh: dp: 32 (over y, z, core), tensor: 4 (over x).
Axes of the slice: x: 4, y: 4, z: 4, core: 2. Of those that a mesh axis runs over, the one named last changes fastest.
Arguments:
- tokens: bfloat16 [4096, 2048], P('dp'), may hold values from -6 to 6
- cotangent: bfloat16 [4096, 2048], P('dp'), may hold values from -6 to 6
- seq_lengths: int32 [4], replicated, may hold values from 1 to 2048, 4096 in all
- stretch_order: int32 [64], replicated, may hold values from 0 to 63, as said below
- attn_gain: float32 [2048], P('dp'), may hold values from 0.5 to 1.5
- w_query: float32 [2048, 16, 128], P('dp', 'tensor'), may hold values from -0.125 to 0.125
- w_key: float32 [2048, 16, 128], P('dp', 'tensor'), may hold values from -0.125 to 0.125
- w_value: float32 [2048, 16, 256], P('dp', 'tensor'), may hold values from -0.125 to 0.125
- w_alpha: float32 [2048, 16], P('dp', 'tensor'), may hold values from -0.125 to 0.125
- w_beta: float32 [2048, 16], P('dp', 'tensor'), may hold values from -0.125 to 0.125
- conv_query: float32 [4, 16, 128], P(None, 'tensor', 'dp'), may hold values from -2.5 to 2.5
- conv_key: float32 [4, 16, 128], P(None, 'tensor', 'dp'), may hold values from -2.5 to 2.5
- conv_value: float32 [4, 16, 256], P(None, 'tensor', 'dp'), may hold values from -2.5 to 2.5
- a_log: float32 [16], P('tensor'), may hold values from -5 to 1.5
- dt_bias: float32 [16], P('tensor'), may hold values from -6 to -2
- head_gain: float32 [256], P('dp'), may hold values from 0.5 to 1.5
- w_outgate: float32 [2048, 16, 256], P('dp', 'tensor'), may hold values from -0.125 to 0.125
- w_output: float32 [16, 256, 2048], P('tensor', None, 'dp'), may hold values from -0.1875 to 0.1875
- mlp_gain: float32 [2048], P('dp'), may hold values from 0.5 to 1.5
- w_gate: float32 [2048, 5504], P('dp', 'tensor'), may hold values from -0.125 to 0.125
- w_up: float32 [2048, 5504], P('dp', 'tensor'), may hold values from -0.125 to 0.125
- w_down: float32 [5504, 2048], P('tensor', 'dp'), may hold values from -0.078125 to 0.078125
Outputs:
- output: bfloat16 [4096, 2048], P('dp', 'tensor')
- d_tokens: bfloat16 [4096, 2048], P('dp', 'tensor')
- d_attn_gain: float32 [2048], P('dp')
- d_w_query: float32 [2048, 16, 128], P('dp', 'tensor')
- d_w_key: float32 [2048, 16, 128], P('dp', 'tensor')
- d_w_value: float32 [2048, 16, 256], P('dp', 'tensor')
- d_w_alpha: float32 [2048, 16], P('dp', 'tensor')
- d_w_beta: float32 [2048, 16], P('dp', 'tensor')
- d_conv_query: float32 [4, 16, 128], P(None, 'tensor', 'dp')
- d_conv_key: float32 [4, 16, 128], P(None, 'tensor', 'dp')
- d_conv_value: float32 [4, 16, 256], P(None, 'tensor', 'dp')
- d_a_log: float32 [16], P('tensor')
- d_dt_bias: float32 [16], P('tensor')
- d_head_gain: float32 [256], P('dp')
- d_w_outgate: float32 [2048, 16, 256], P('dp', 'tensor')
- d_w_output: float32 [16, 256, 2048], P('tensor', None, 'dp')
- d_mlp_gain: float32 [2048], P('dp')
- d_w_gate: float32 [2048, 5504], P('dp', 'tensor')
- d_w_up: float32 [2048, 5504], P('dp', 'tensor')
- d_w_down: float32 [5504, 2048], P('tensor', 'dp')
Inputs may be any that keep to these rules, and one draw needn't show every extreme that they name: `seq_lengths`: sum to 4096; the longest is exactly 2048. `stretch_order`: names each of the 64 blocks once; at least one block arrives 64 // 2 blocks away, counted round, from its place.
All inputs are finite; a program needn't handle non-finite values.
Results may differ from a plain program's by a relative error of at most 0.03.
Values may be sent and summed in bfloat16 or wider, within the bound.
A program may use at most 256 MiB of HBM per device.

v0:
```python
from functools import partial
import math

import jax
import jax.numpy as jnp
from jax import lax
from jax.sharding import Mesh
from jax.sharding import PartitionSpec as P

STRETCH = 64
DP = ("dp_0", "dp_1", "dp_2")


EPSILON = 1e-06
MAXIMUM_ACCURACY = lax.Precision.HIGHEST


def side_by_side(arrays, axis, dim, along):
    ends, at = ([], 0)
    for a in arrays[:-1]:
        at += a.shape[along]
        ends.append(at)
    both = jnp.concatenate(arrays, axis=along)
    return tuple(jnp.split(lax.all_gather(both, axis, axis=dim, tiled=True), ends, axis=along))


def side_by_side_2(arrays, axis, dim, along):
    widths = [math.prod(a.shape[along:]) for a in arrays]
    both = jnp.concatenate(
        [a.reshape(*a.shape[:along], w) for a, w in zip(arrays, widths)], axis=along
    )
    whole = lax.all_gather(both, axis, axis=dim, tiled=True)
    blocks = jnp.split(whole, [sum(widths[:k]) for k in range(1, len(widths))], axis=along)
    return tuple(
        (b.reshape(*whole.shape[:along], *a.shape[along:]) for a, b in zip(arrays, blocks))
    )


def from_behind(value, axis, steps):
    count = lax.axis_size(axis)
    initial, last = (max(0, -steps), min(count, count - steps))
    return lax.ppermute(value, axis, [(source, source + steps) for source in range(initial, last)])


def carried_in(x, axis, join, neutral):
    place = lax.axis_index(axis)
    gathered = jax.tree.map(
        lambda a, kind: lax.all_gather(a.astype(kind), axis), x, (jnp.bfloat16, jnp.bfloat16)
    )
    state = jax.tree.map(lambda a, e: jnp.zeros_like(a) + jnp.asarray(e, a.dtype), x, neutral)

    def one(turn, state):
        return join(
            state,
            jax.tree.map(
                lambda a, own: lax.dynamic_index_in_dim(a, turn, 0, False).astype(own.dtype),
                gathered,
                x,
            ),
        )

    return lax.fori_loop(0, place, one, state)


def sent_to_all(x, axis):
    peers = lax.axis_size(axis)
    return lax.all_to_all(jnp.broadcast_to(x[None], (peers, *x.shape)), axis, 0, 0, tiled=True)


def over_copies(x, axis):
    return sent_to_all(x, axis).astype(jnp.float32).sum(axis=0)


def nothing_yet(x, identity):
    return jax.tree.map(
        lambda part, zero: jnp.zeros_like(part) + jnp.asarray(zero, part.dtype), x, identity
    )


def entering(x, axes, combine, identity):
    before = start = nothing_yet(x, identity)
    subtotal = x
    for axis in reversed(axes):
        peers, here = (lax.axis_size(axis), lax.axis_index(axis))
        pieces = jax.tree.map(
            lambda part, kind: lax.all_gather(part.astype(kind), axis),
            subtotal,
            jax.tree.map(lambda a: jnp.bfloat16 if a.dtype == jnp.float32 else a.dtype, x),
        )
        inside, subtotal = (start, start)
        for k in reversed(range(peers)):
            passed = k > here
            subtotal = combine(
                subtotal, jax.tree.map(lambda part, own: part[k].astype(own.dtype), pieces, x)
            )
            inside = jax.tree.map(lambda new, old: jnp.where(passed, new, old), subtotal, inside)
        before = combine(inside, before)
    return before


def in_one_piece(arrays, axis, dim, along):
    columns = [a.reshape(*a.shape[:along], -1) for a in arrays]
    both = jnp.concatenate(columns, axis=along)
    whole, at, outs = (lax.psum_scatter(both, axis, scatter_dimension=dim, tiled=True), 0, [])
    for a, column in zip(arrays, columns):
        slab = whole[..., at : at + column.shape[along]]
        outs.append(slab.reshape(*slab.shape[:along], *a.shape[along:]))
        at += column.shape[along]
    return tuple(outs)


def in_one_piece_2(arrays, axis, dim, along):
    both = jnp.concatenate(arrays, axis=along)
    whole, at, outs = (lax.psum_scatter(both, axis, scatter_dimension=dim, tiled=True), 0, [])
    for a in arrays:
        outs.append(lax.slice_in_dim(whole, at, at + a.shape[along], axis=along))
        at += a.shape[along]
    return tuple(outs)


def taken_together(x, axis):
    everything = sent_to_all(x, axis)
    return jnp.sum(everything, axis=0)


def packed_total(arrays, axis):
    line, at, outs = (jnp.concatenate([a.reshape(-1) for a in arrays]), 0, [])
    subtotal = taken_together(line, axis)
    for a in arrays:
        outs.append(subtotal[at : at + a.size].reshape(a.shape))
        at += a.size
    return tuple(outs)


def rms_norm(inputs, gain_vector):
    return (
        inputs
        * lax.rsqrt(jnp.mean(inputs * inputs, axis=-1, keepdims=True) + EPSILON)
        * gain_vector
    )


def swiglu(gate_values, upward):
    return jax.nn.silu(gate_values) * upward


def gate_norm(mixed_out, gate_pre, gain_vector):
    gate_values = gate_pre.reshape(mixed_out.shape)
    normed = (
        mixed_out
        * lax.rsqrt(jnp.mean(mixed_out * mixed_out, axis=-1, keepdims=True) + EPSILON)
        * gain_vector
        * jax.nn.silu(gate_values)
    )
    return normed.reshape(mixed_out.shape[0], -1)


def rounded(values):
    return lax.optimization_barrier(values.astype(jnp.bfloat16)).astype(jnp.float32)


def bf_dot(former, latter):
    return jnp.dot(former, latter, preferred_element_type=jnp.float32)


def dot_back(former, latter):
    return lax.dot_general(
        former, latter, (((1,), (1,)), ((), ())), preferred_element_type=jnp.float32
    )


def dot_grad(former, latter):
    return lax.dot_general(
        former, latter, (((0,), (0,)), ((), ())), preferred_element_type=jnp.float32
    )


def heads_first(values, stretch_slots):
    return values.reshape(
        (stretch_slots, values.shape[0] // stretch_slots) + values.shape[1:]
    ).swapaxes(1, 2)


def causal_filter(current, before, weight, valid_taps):
    filter_taps = weight.shape[0]
    length = current.shape[0]
    extended = jnp.concatenate([before, current], axis=0)
    summed = jnp.zeros_like(current)
    for tap_index in range(filter_taps):
        summed = (
            summed
            + valid_taps[:, tap_index : tap_index + 1]
            * weight[tap_index]
            * extended[tap_index : tap_index + length]
        )
    return jax.nn.silu(summed)


def unit_heads(values, heads_count, factor):
    shaped = values.reshape(values.shape[0], heads_count, -1)
    return shaped * lax.rsqrt(jnp.sum(shaped * shaped, axis=-1, keepdims=True) + EPSILON) * factor


def mix_inputs(
    valid_taps,
    query_pre,
    key_pre,
    value_pre,
    edge_rows,
    alpha_pre,
    beta_pre,
    filter_query,
    filter_key,
    filter_value,
    a_log,
    dt_bias,
):
    heads_count = alpha_pre.shape[1]
    split_one = query_pre.shape[1]
    split_two = split_one + key_pre.shape[1]
    queries = unit_heads(
        causal_filter(query_pre, edge_rows[:, :split_one], filter_query, valid_taps),
        heads_count,
        (split_one // heads_count) ** (-0.5),
    )
    key_rows = unit_heads(
        causal_filter(key_pre, edge_rows[:, split_one:split_two], filter_key, valid_taps),
        heads_count,
        1.0,
    )
    value_rows = causal_filter(
        value_pre, edge_rows[:, split_two:], filter_value, valid_taps
    ).reshape(value_pre.shape[0], heads_count, -1)
    beta_rows = jax.nn.sigmoid(beta_pre)
    decays = -jnp.exp(a_log) * jax.nn.softplus(alpha_pre + dt_bias)
    return (queries, key_rows, value_rows, beta_rows, decays)


def decay_table(cumulative, mask_table):
    spread = cumulative[..., :, None] - cumulative[..., None, :]
    return jnp.exp(jnp.where(mask_table > 0.0, spread, 0.0)) * mask_table


def prepare(stretch_masks, key_rows, value_rows, beta_rows, decays):
    carried, closing, strict_mask, incl_mask = stretch_masks
    stretch_slots = carried.shape[0]
    key_t = heads_first(key_rows, stretch_slots)
    value_t = heads_first(value_rows, stretch_slots)
    beta_t = heads_first(beta_rows, stretch_slots)
    cumulative = jnp.cumsum(heads_first(decays, stretch_slots), axis=-1)
    stretch_span = key_t.shape[2]
    key_depth = key_t.shape[3]
    key_gram = jnp.einsum("nhik,nhjk->nhij", key_t, key_t, precision=MAXIMUM_ACCURACY)
    system = jnp.eye(stretch_span, dtype=jnp.float32) + beta_t[
        ..., :, None
    ] * key_gram * decay_table(cumulative, strict_mask)
    lead_rows = (beta_t * jnp.exp(cumulative) * carried[:, None, :])[..., None] * key_t
    right_side = jnp.concatenate([lead_rows, beta_t[..., None] * value_t], axis=-1)
    solved = jax.scipy.linalg.solve_triangular(system, right_side, lower=True, unit_diagonal=True)
    w_part = solved[..., :key_depth]
    u_part = solved[..., key_depth:]
    tail_decay = jnp.exp(cumulative[..., -1:] - cumulative) * closing[:, None, :]
    key_tail = key_t * tail_decay[..., None]
    carry_keep = jnp.exp(cumulative[..., -1]) * carried[:, None, -1]
    handoff_between = carry_keep[..., None, None] * jnp.eye(
        key_depth, dtype=jnp.float32
    ) - jnp.einsum("nhjk,nhjl->nhkl", key_tail, w_part, precision=MAXIMUM_ACCURACY)
    inject = jnp.einsum("nhjk,nhjv->nhkv", key_tail, u_part, precision=MAXIMUM_ACCURACY)
    return (cumulative, w_part, u_part, handoff_between, inject)


def emit_outputs(
    stretch_masks, queries, key_rows, cumulative, w_part, u_part, handoff_between, inject, state_in
):
    carried, closing, strict_mask, incl_mask = stretch_masks
    stretch_slots = carried.shape[0]
    starts = []
    current_state = state_in
    for segment_index in range(stretch_slots):
        starts.append(current_state)
        current_state = (
            jnp.einsum(
                "wsz,wzp->wsp",
                handoff_between[segment_index],
                current_state,
                precision=MAXIMUM_ACCURACY,
            )
            + inject[segment_index]
        )
    entry_states = jnp.stack(starts)
    query_t = heads_first(queries, stretch_slots)
    key_t = heads_first(key_rows, stretch_slots)
    fresh_values = u_part - jnp.einsum(
        "nhck,nhkv->nhcv", w_part, entry_states, precision=MAXIMUM_ACCURACY
    )
    weights = jnp.einsum(
        "nhik,nhjk->nhij", query_t, key_t, precision=MAXIMUM_ACCURACY
    ) * decay_table(cumulative, incl_mask)
    decayed = query_t * (jnp.exp(cumulative) * carried[:, None, :])[..., None]
    mixed_out = jnp.einsum(
        "nhik,nhkv->nhiv", decayed, entry_states, precision=MAXIMUM_ACCURACY
    ) + jnp.einsum("nhij,nhjv->nhiv", weights, fresh_values, precision=MAXIMUM_ACCURACY)
    return (mixed_out.swapaxes(1, 2).reshape(queries.shape[0], queries.shape[1], -1), current_state)


def compose(preceding_pieces, successor_piece):
    return (
        jnp.einsum(
            "hkl,hlm->hkm", successor_piece[0], preceding_pieces[0], precision=MAXIMUM_ACCURACY
        ),
        jnp.einsum(
            "wsz,wzp->wsp", successor_piece[0], preceding_pieces[1], precision=MAXIMUM_ACCURACY
        )
        + successor_piece[1],
    )


def views(fetched, model_width):
    return (
        fetched[1].reshape(model_width, -1),
        fetched[2].reshape(model_width, -1),
        fetched[3].reshape(model_width, -1),
        fetched[4],
        fetched[5],
        fetched[10].reshape(model_width, -1),
        fetched[11].reshape(-1, model_width),
        fetched[13],
        fetched[14],
        fetched[15],
    )


def body(
    tokens,
    cotangent,
    seq_lengths,
    stretch_order,
    attn_gain,
    w_query,
    w_key,
    w_value,
    w_alpha,
    w_beta,
    conv_query,
    conv_key,
    conv_value,
    a_log,
    dt_bias,
    head_gain,
    w_outgate,
    w_output,
    mlp_gain,
    w_gate,
    w_up,
    w_down,
):
    device = lax.axis_index(DP)
    tensor_rank = lax.axis_index("tensor")
    length, model_width = tokens.shape
    stretch_slots = length // STRETCH
    local_heads = a_log.shape[0]
    key_depth = w_query.shape[2]
    value_depth = w_value.shape[2]
    pieces = side_by_side((tokens, cotangent), DP, 0, 1)
    blocks = pieces[0].shape[0] // STRETCH
    wanted = device * stretch_slots + jnp.arange(stretch_slots, dtype=jnp.int32)
    select = (wanted[:, None] == stretch_order[None, :]).astype(jnp.bfloat16)
    owned_input, owned_upstream = tuple(
        (
            jnp.einsum(
                "oj,jrd->ord",
                select,
                fragment.reshape(blocks, STRETCH, -1),
                preferred_element_type=jnp.float32,
            )
            for fragment in pieces
        )
    )
    inputs = owned_input.reshape(length, model_width)
    upstream = owned_upstream.reshape(length, model_width)
    fetched = (
        *side_by_side_2(
            (
                attn_gain.astype(jnp.bfloat16),
                w_query.astype(jnp.bfloat16),
                w_key.astype(jnp.bfloat16),
                w_value.astype(jnp.bfloat16),
                w_alpha.astype(jnp.bfloat16),
                w_beta.astype(jnp.bfloat16),
            ),
            DP,
            0,
            1,
        ),
        *side_by_side((conv_query.astype(jnp.bfloat16), conv_key.astype(jnp.bfloat16)), DP, 2, 0),
        lax.all_gather(conv_value.astype(jnp.bfloat16), DP, axis=2, tiled=True),
        lax.all_gather(head_gain.astype(jnp.bfloat16), DP, axis=0, tiled=True),
        lax.all_gather(w_outgate.astype(jnp.bfloat16), DP, axis=0, tiled=True),
        lax.all_gather(w_output.astype(jnp.bfloat16), DP, axis=2, tiled=True),
        *side_by_side_2(
            (mlp_gain.astype(jnp.bfloat16), w_gate.astype(jnp.bfloat16), w_up.astype(jnp.bfloat16)),
            DP,
            0,
            1,
        ),
        lax.all_gather(w_down.astype(jnp.bfloat16), DP, axis=1, tiled=True),
    )
    (
        flat_query,
        flat_key,
        flat_value,
        flat_alpha,
        flat_beta,
        flat_gate,
        flat_output,
        mlp_gate,
        mlp_up,
        mlp_down,
    ) = views(fetched, model_width)
    filter_taps = fetched[6].shape[0]
    positions = device * length + jnp.arange(length, dtype=jnp.int32)
    seq_ends = jnp.cumsum(seq_lengths, dtype=jnp.int32)
    begins = seq_ends - seq_lengths
    inside = (positions[:, None] >= begins[None, :]) & (positions[:, None] < seq_ends[None, :])
    seq_begin = jnp.sum(jnp.where(inside, begins[None, :], 0), axis=1, dtype=jnp.int32)
    valid_taps = (
        positions[:, None] - (filter_taps - 1) + jnp.arange(filter_taps, dtype=jnp.int32)[None, :]
        >= seq_begin[:, None]
    ).astype(jnp.float32)
    stretch_begin = seq_begin.reshape(stretch_slots, STRETCH)
    stretch_first = positions.reshape(stretch_slots, STRETCH)[:, :1]
    carried = (stretch_begin < stretch_first).astype(jnp.float32)
    closing = (stretch_begin == stretch_begin[:, -1:]).astype(jnp.float32)
    same_seq = stretch_begin[:, :, None] == stretch_begin[:, None, :]
    order_rows = jnp.arange(STRETCH, dtype=jnp.int32)[:, None]
    order_cols = jnp.arange(STRETCH, dtype=jnp.int32)[None, :]
    strict_mask = (same_seq & (order_rows > order_cols)).astype(jnp.float32)[:, None]
    incl_mask = (same_seq & (order_rows >= order_cols)).astype(jnp.float32)[:, None]
    stretch_masks = (carried, closing, strict_mask, incl_mask)
    normed_one, norm_one_back = jax.vjp(rms_norm, inputs, fetched[0].astype(jnp.float32))
    normed_low = normed_one.astype(jnp.bfloat16)
    query_pre = bf_dot(normed_low, flat_query)
    key_pre = bf_dot(normed_low, flat_key)
    value_pre = bf_dot(normed_low, flat_value)
    gate_pre = bf_dot(normed_low, flat_gate)
    alpha_pre = bf_dot(normed_low, flat_alpha)
    beta_pre = bf_dot(normed_low, flat_beta)
    tail_rows = jnp.concatenate(
        [
            query_pre[length - filter_taps + 1 :],
            key_pre[length - filter_taps + 1 :],
            value_pre[length - filter_taps + 1 :],
        ],
        axis=1,
    )
    edge_rows = from_behind(tail_rows, DP, 1)
    mixed_in, mix_back = jax.vjp(
        partial(mix_inputs, valid_taps),
        query_pre,
        key_pre,
        value_pre,
        edge_rows,
        alpha_pre,
        beta_pre,
        fetched[6].astype(jnp.float32).reshape(filter_taps, -1),
        fetched[7].astype(jnp.float32).reshape(filter_taps, -1),
        fetched[8].astype(jnp.float32).reshape(filter_taps, -1),
        a_log,
        dt_bias,
    )
    queries_low = rounded(mixed_in[0])
    keys_low = rounded(mixed_in[1])
    values_low = rounded(mixed_in[2])
    prepared, prepare_back = jax.vjp(
        partial(prepare, stretch_masks), keys_low, values_low, mixed_in[3], mixed_in[4]
    )
    cumulative, w_part, u_part, handoff_between, inject = prepared
    eye_keys = jnp.broadcast_to(
        jnp.eye(key_depth, dtype=jnp.float32), (local_heads, key_depth, key_depth)
    )
    zero_state = jnp.zeros((local_heads, key_depth, value_depth), jnp.float32)
    device_transit = eye_keys
    insert_on_device = zero_state
    for segment_index in range(stretch_slots):
        insert_on_device = (
            jnp.einsum(
                "wsz,wzp->wsp",
                handoff_between[segment_index],
                insert_on_device,
                precision=MAXIMUM_ACCURACY,
            )
            + inject[segment_index]
        )
        device_transit = jnp.einsum(
            "hkl,hlm->hkm",
            handoff_between[segment_index],
            device_transit,
            precision=MAXIMUM_ACCURACY,
        )
    prefix = carried_in((device_transit, insert_on_device), DP, compose, (eye_keys, zero_state))
    state_in = prefix[1]
    emitted, emit_back = jax.vjp(
        partial(emit_outputs, stretch_masks),
        queries_low,
        keys_low,
        cumulative,
        w_part,
        u_part,
        handoff_between,
        inject,
        state_in,
    )
    mixed_out = emitted[0]
    head_flat, gate_norm_back = jax.vjp(
        gate_norm, mixed_out, gate_pre, fetched[9].astype(jnp.float32)
    )
    head_low = head_flat.astype(jnp.bfloat16)
    attn_out = over_copies(bf_dot(head_low, flat_output).astype(jnp.bfloat16), "tensor").astype(
        jnp.float32
    )
    middle = inputs + attn_out
    normed_two, norm_two_back = jax.vjp(rms_norm, middle, fetched[12].astype(jnp.float32))
    normed_two_low = normed_two.astype(jnp.bfloat16)
    gate_mlp = bf_dot(normed_two_low, mlp_gate)
    up_mlp = bf_dot(normed_two_low, mlp_up)
    hidden, swiglu_back = jax.vjp(swiglu, gate_mlp, up_mlp)
    hidden_low = hidden.astype(jnp.bfloat16)
    mlp_out = over_copies(bf_dot(hidden_low, mlp_down).astype(jnp.bfloat16), "tensor").astype(
        jnp.float32
    )
    result = middle + mlp_out
    upstream_low = upstream.astype(jnp.bfloat16)
    d_hidden = dot_back(upstream_low, mlp_down)
    grad_down = dot_grad(hidden_low, upstream_low)
    d_gate_mlp, d_up_mlp = swiglu_back(d_hidden)
    gate_grad_low = d_gate_mlp.astype(jnp.bfloat16)
    up_grad_low = d_up_mlp.astype(jnp.bfloat16)
    grad_gate = dot_grad(normed_two_low, gate_grad_low)
    grad_up = dot_grad(normed_two_low, up_grad_low)
    d_normed_two = over_copies(
        (dot_back(gate_grad_low, mlp_gate) + dot_back(up_grad_low, mlp_up)).astype(jnp.bfloat16),
        "tensor",
    ).astype(jnp.float32)
    d_middle_norm, grad_gain_two = norm_two_back(d_normed_two)
    d_middle = upstream + d_middle_norm
    middle_low = d_middle.astype(jnp.bfloat16)
    d_head = dot_back(middle_low, flat_output)
    grad_output = dot_grad(head_low, middle_low)
    d_mixed, d_gate_pre, grad_head_part = gate_norm_back(d_head)
    first_pass = emit_back((d_mixed, zero_state))
    suffix = entering(
        (jnp.swapaxes(device_transit, 1, 2), first_pass[7]), DP, compose, (eye_keys, zero_state)
    )
    second_pass = emit_back((jnp.zeros_like(d_mixed), suffix[1]))
    emit_grads = jax.tree.map(jnp.add, first_pass, second_pass)
    prep_grads = prepare_back(
        (emit_grads[2], emit_grads[3], emit_grads[4], emit_grads[5], emit_grads[6])
    )
    mix_grads = mix_back(
        (emit_grads[0], emit_grads[1] + prep_grads[0], prep_grads[1], prep_grads[2], prep_grads[3])
    )
    (
        d_query_pre,
        d_key_pre,
        d_value_pre,
        d_edge,
        d_alpha_pre,
        d_beta_pre,
        grad_filter_query,
        grad_filter_key,
        grad_filter_value,
        grad_a_log,
        grad_dt_bias,
    ) = mix_grads
    back_edge = from_behind(d_edge, DP, -1)
    back_full = jnp.pad(back_edge, ((length - filter_taps + 1, 0), (0, 0)))
    split_one = d_query_pre.shape[1]
    split_two = split_one + d_key_pre.shape[1]
    d_query_pre = d_query_pre + back_full[:, :split_one]
    d_key_pre = d_key_pre + back_full[:, split_one:split_two]
    d_value_pre = d_value_pre + back_full[:, split_two:]
    query_grad_low = d_query_pre.astype(jnp.bfloat16)
    key_grad_low = d_key_pre.astype(jnp.bfloat16)
    value_grad_low = d_value_pre.astype(jnp.bfloat16)
    outgate_grad_low = d_gate_pre.astype(jnp.bfloat16)
    alpha_grad_low = d_alpha_pre.astype(jnp.bfloat16)
    beta_grad_low = d_beta_pre.astype(jnp.bfloat16)
    d_normed_part = (
        dot_back(query_grad_low, flat_query)
        + dot_back(key_grad_low, flat_key)
        + dot_back(value_grad_low, flat_value)
    )
    d_normed_part = (
        d_normed_part
        + dot_back(outgate_grad_low, flat_gate)
        + dot_back(alpha_grad_low, flat_alpha)
        + dot_back(beta_grad_low, flat_beta)
    )
    d_normed_one, grad_head_gain = (
        over_copies(d_normed_part.astype(jnp.bfloat16), "tensor").astype(jnp.float32),
        over_copies(grad_head_part.astype(jnp.bfloat16), "tensor").astype(jnp.float32),
    )
    d_inputs_norm, grad_gain_one = norm_one_back(d_normed_one)
    d_inputs = d_middle + d_inputs_norm
    scattered = (
        *tuple(
            (
                part.astype(jnp.float32)
                for part in in_one_piece(
                    (
                        grad_gain_one.astype(jnp.bfloat16),
                        dot_grad(normed_low, query_grad_low)
                        .reshape(model_width, local_heads, -1)
                        .astype(jnp.bfloat16),
                        dot_grad(normed_low, key_grad_low)
                        .reshape(model_width, local_heads, -1)
                        .astype(jnp.bfloat16),
                        dot_grad(normed_low, value_grad_low)
                        .reshape(model_width, local_heads, -1)
                        .astype(jnp.bfloat16),
                        dot_grad(normed_low, alpha_grad_low).astype(jnp.bfloat16),
                        dot_grad(normed_low, beta_grad_low).astype(jnp.bfloat16),
                    ),
                    DP,
                    0,
                    1,
                )
            )
        ),
        *tuple(
            (
                part.astype(jnp.float32)
                for part in in_one_piece_2(
                    (
                        grad_filter_query.reshape(filter_taps, local_heads, -1).astype(
                            jnp.bfloat16
                        ),
                        grad_filter_key.reshape(filter_taps, local_heads, -1).astype(jnp.bfloat16),
                    ),
                    DP,
                    2,
                    0,
                )
            )
        ),
        lax.psum_scatter(
            grad_filter_value.reshape(filter_taps, local_heads, -1).astype(jnp.bfloat16),
            DP,
            scatter_dimension=2,
            tiled=True,
        ).astype(jnp.float32),
        lax.psum_scatter(
            grad_head_gain.astype(jnp.bfloat16), DP, scatter_dimension=0, tiled=True
        ).astype(jnp.float32),
        lax.psum_scatter(
            dot_grad(normed_low, outgate_grad_low)
            .reshape(model_width, local_heads, -1)
            .astype(jnp.bfloat16),
            DP,
            scatter_dimension=0,
            tiled=True,
        ).astype(jnp.float32),
        lax.psum_scatter(
            grad_output.reshape(local_heads, -1, model_width).astype(jnp.bfloat16),
            DP,
            scatter_dimension=2,
            tiled=True,
        ).astype(jnp.float32),
        *tuple(
            (
                part.astype(jnp.float32)
                for part in in_one_piece(
                    (
                        grad_gain_two.astype(jnp.bfloat16),
                        grad_gate.astype(jnp.bfloat16),
                        grad_up.astype(jnp.bfloat16),
                    ),
                    DP,
                    0,
                    1,
                )
            )
        ),
        lax.psum_scatter(
            grad_down.astype(jnp.bfloat16), DP, scatter_dimension=1, tiled=True
        ).astype(jnp.float32),
    )
    head_sums = packed_total((grad_a_log, grad_dt_bias), DP)
    quarter = model_width // lax.axis_size("tensor")
    result_cols = lax.dynamic_slice_in_dim(result, tensor_rank * quarter, quarter, 1).astype(
        jnp.bfloat16
    )
    dinput_cols = lax.dynamic_slice_in_dim(d_inputs, tensor_rank * quarter, quarter, 1).astype(
        jnp.bfloat16
    )
    pieces = side_by_side((result_cols, dinput_cols), DP, 0, 1)
    blocks = pieces[0].shape[0] // STRETCH
    mine = lax.dynamic_slice_in_dim(stretch_order, device * stretch_slots, stretch_slots)
    present = jnp.arange(blocks, dtype=jnp.int32)
    select = (mine[:, None] == present[None, :]).astype(jnp.bfloat16)
    out_rows, grad_rows = tuple(
        (
            jnp.einsum(
                "oj,jrd->ord",
                select,
                fragment.reshape(blocks, STRETCH, -1),
                preferred_element_type=jnp.float32,
            )
            for fragment in pieces
        )
    )
    return (
        out_rows.reshape(length, quarter).astype(jnp.bfloat16),
        grad_rows.reshape(length, quarter).astype(jnp.bfloat16),
        scattered[0],
        scattered[1],
        scattered[2],
        scattered[3],
        scattered[4],
        scattered[5],
        scattered[6],
        scattered[7],
        scattered[8],
        head_sums[0],
        head_sums[1],
        scattered[9],
        scattered[10],
        scattered[11],
        scattered[12],
        scattered[13],
        scattered[14],
        scattered[15],
    )


def solution(mesh):
    torus = Mesh(
        mesh.devices.reshape(4, 4, 2, mesh.shape["tensor"]), ("dp_0", "dp_1", "dp_2", "tensor")
    )
    in_specs = (
        P(DP, None),
        P(DP, None),
        P(),
        P(),
        P(DP),
        P(DP, "tensor", None),
        P(DP, "tensor", None),
        P(DP, "tensor", None),
        P(DP, "tensor"),
        P(DP, "tensor"),
        P(None, "tensor", DP),
        P(None, "tensor", DP),
        P(None, "tensor", DP),
        P("tensor"),
        P("tensor"),
        P(DP),
        P(DP, "tensor", None),
        P("tensor", None, DP),
        P(DP),
        P(DP, "tensor"),
        P(DP, "tensor"),
        P("tensor", DP),
    )
    out_specs = (
        P(DP, "tensor"),
        P(DP, "tensor"),
        P(DP),
        P(DP, "tensor", None),
        P(DP, "tensor", None),
        P(DP, "tensor", None),
        P(DP, "tensor"),
        P(DP, "tensor"),
        P(None, "tensor", DP),
        P(None, "tensor", DP),
        P(None, "tensor", DP),
        P("tensor"),
        P("tensor"),
        P(DP),
        P(DP, "tensor", None),
        P("tensor", None, DP),
        P(DP),
        P(DP, "tensor"),
        P(DP, "tensor"),
        P("tensor", DP),
    )
    return jax.shard_map(body, mesh=torus, in_specs=in_specs, out_specs=out_specs, check_vma=False)
```

profile of v0, /device:TPU:1, one launch (start us, length us, event | category | flops | bytes accessed | tf_op | source)
XLA Modules:
  0.0 1246.1 jit_solution(17257847896966626555)
XLA Ops:
  20.8 27.4 %all_gather.79 = bf16[8,4,128]{0,1,2:T(4,128)(2,1)S(1)} all-gather(bf16[8,4,4]{0,1,2:T(4,128)(2,1)S(1)} %pad_maximum_fusion.14), channel_id=1, replica_groups=mesh['dp_0'=4,'dp_1'=4,'dp_2'=2,'tensor'=4] {'dp_0','dp_1','dp_2'}, dimensions={2}, use_global_device_ids=true | all-gather | bytes 8448 | tf_op jit(solution)/shard_map/all_gather | solution.py:24
  54.4 24.2 %all_gather.81 = bf16[4,4,256]{1,0,2:T(4,128)(2,1)S(1)} all-gather(bf16[4,4,8]{1,0,2:T(4,128)(2,1)S(1)} %copy.691), channel_id=1, replica_groups=mesh['dp_0'=4,'dp_1'=4,'dp_2'=2,'tensor'=4] {'dp_0','dp_1','dp_2'}, dimensions={2}, use_global_device_ids=true | all-gather | bytes 8448 | tf_op jit(solution)/shard_map/all_gather | solution.py:396
  84.6 103.2 %all-gather.20.cloned.1.call-done = bf16[4096,4096]{1,0:T(8,128)(2,1)} async-done(((bf16[128,4096]{1,0:T(8,128)(2,1)}), bf16[4096,4096]{1,0:T(8,128)(2,1)}) %all-gather.20.cloned.1.call-update) | async-done | bytes 33554448 | tf_op jit(solution)/shard_map/all_gather | solution.py:24
  187.8 18.5 %fusion.402 = (bf16[4096,2048]{1,0:T(8,128)(2,1)S(1)}, bf16[4096,2048]{1,0:T(8,128)(2,1)}) fusion(bf16[4096,4096]{1,0:T(8,128)(2,1)} %all-gather.20.cloned.1.call-done), kind=kLoop, calls=%fused_computation.664 | loop fusion | bytes 67108864 | tf_op jit(solution)/shard_map/split | solution.py:24
  206.2 21.3 %multiply_reduce_fusion.5 = (f32[2,64]{0,1:T(8,128)}, f32[2,64,2048]{2,0,1:T(2,128)S(1)}) fusion(bf16[64,64,2048]{2,1,0:T(8,128)(2,1)S(1)} %bitcast.557, s32[64]{0:T(128)} %param.27, s32[2]{0:T(128)} %iota_add_fusion.2), kind=kOutput, calls=%fused_computation.133 | convolution fusion | flops 34078720 | bytes 17826568 | tf_op jit(solution)/shard_map/oj,jrd->ord/dot_general | solution.py:370
  251.2 39.3 %custom-call.10 = f32[2,4,1,64,64]{3,4,2,1,0:T(8,128)S(1)} custom-call(f32[2,4,1,64,64]{4,3,2,1,0:T(8,128)S(1)} %fusion.148), custom_call_target="InvertDiagBlocksLowerTriangular" | custom-call | tf_op jit(solution)/shard_map/jvp(jit(_solve_triangular))/vmap(vmap())/triangular_solve | solution.py:259
  316.3 62.4 %all-reduce.39 = bf16[256]{0:T(256)(128)(2,1)S(1)} all-reduce(bf16[256]{0:T(256)(128)(2,1)S(1)} %dynamic-update-slice), channel_id=1, replica_groups=mesh['dp_0'=4,'dp_1'=4,'dp_2'=2,'tensor'=4] {'dp_0','dp_1','dp_2'}, use_global_device_ids=true, to_apply=%add.39 | all-reduce | flops 256 | bytes 1024
  386.2 14.6 %all-gather.36.cloned.1.call-done = bf16[128,128,256]{2,1,0:T(8,128)(2,1)} async-done(((bf16[4,128,256]{2,1,0:T(8,128)(2,1)}), bf16[128,128,256]{2,1,0:T(8,128)(2,1)}) %all-gather.36.cloned.1.call-update) | async-done | bytes 8388624 | tf_op jit(solution)/shard_map/all_gather | solution.py:48
  412.4 37.1 %all-gather.26.cloned.1.call-done = bf16[4,256,2048]{1,2,0:T(8,128)(2,1)} async-done(((bf16[4,256,64]{1,2,0:T(8,128)(2,1)}), bf16[4,256,2048]{1,2,0:T(8,128)(2,1)}) %all-gather.26.cloned.1.call-update) | async-done | bytes 4194320 | tf_op jit(solution)/shard_map/all_gather | solution.py:399
  459.6 52.5 %all-gather.28.cloned.1.call-done = bf16[2048,2753]{1,0:T(8,128)(2,1)} async-done(((bf16[64,2753]{1,0:T(8,128)(2,1)}), bf16[2048,2753]{1,0:T(8,128)(2,1)}) %all-gather.28.cloned.1.call-update) | async-done | bytes 11276304 | tf_op jit(solution)/shard_map/all_gather | solution.py:32
  514.0 23.6 %fusion.3 = f32[2,64,2048]{2,0,1:T(2,128)S(1)} fusion(bf16[64,64,2048]{2,1,0:T(8,128)(2,1)} %bitcast.535, s32[64]{0:T(128)S(1)} %copy-done.212, s32[2]{0:T(128)S(1)} %copy-done.214), kind=kOutput, calls=%fused_computation.4 | convolution fusion | flops 33554560 | bytes 17826056 | tf_op jit(solution)/shard_map/oj,jrd->ord/dot_general | solution.py:370
  539.2 23.1 %all-gather.30.cloned.1.call-done = bf16[1376,2048]{0,1:T(8,128)(2,1)} async-done(((bf16[1376,64]{0,1:T(8,128)(2,1)}), bf16[1376,2048]{0,1:T(8,128)(2,1)}) %all-gather.30.cloned.1.call-update) | async-done | bytes 5636112 | tf_op jit(solution)/shard_map/all_gather | solution.py:406
  585.6 8.6 multiply_convert_fusion.4
  609.4 23.9 %all-to-all-done.2 = bf16[4,128,2048]{2,1,0:T(8,128)(2,1)} async-done(((bf16[4,128,2048]{2,1,0:T(8,128)(2,1)}), bf16[4,128,2048]{2,1,0:T(8,128)(2,1)}, u32[]{:S(2)}, u32[]{:S(2)}) %all-to-all-start.2) | async-done | bytes 2097184 | tf_op jit(solution)/shard_map/all_to_all | solution.py:67
  657.3 12.7 %all-gather.3 = bf16[16,128,128]{2,1,0:T(8,128)(2,1)S(1)} all-gather(bf16[4,128,128]{2,1,0:T(8,128)(2,1)S(1)} %get-tuple-element.381), channel_id=5, replica_groups=mesh['dp_0'=4,'dp_1'=4,'dp_2'=2,'tensor'=4] {'dp_1'}, dimensions={0}, use_global_device_ids=true | all-gather | bytes 655360 | tf_op jit(solution)/shard_map/all_gather | solution.py:86
  719.7 55.9 %concatenate.55 = bf16[2048,2753]{0,1:T(8,128)(2,1)} concatenate(bf16[2048,1]{0,1:T(2,128)(2,1)S(1)} %convert_element_type.651, bf16[2048,1376]{0,1:T(8,128)(2,1)} %convolution_convert_fusion.1, bf16[2048,1376]{0,1:T(8,128)(2,1)} %convolution_convert_fusion), dimensions={1} | concatenate | bytes 22552576 | tf_op jit(solution)/shard_map/concatenate | solution.py:103
  775.6 15.9 %copy.792 = bf16[2048,2753]{1,0:T(8,128)(2,1)} copy(bf16[2048,2753]{0,1:T(8,128)(2,1)} %concatenate.55) | data formatting | bytes 22552576
  792.4 12.3 all-gather.4
  907.6 16.8 %all-to-all-done.3 = bf16[4,128,2048]{2,1,0:T(8,128)(2,1)} async-done(((bf16[4,128,2048]{2,1,0:T(8,128)(2,1)}), bf16[4,128,2048]{2,1,0:T(8,128)(2,1)}, u32[]{:S(2)}, u32[]{:S(2)}) %all-to-all-start.3) | async-done | bytes 2097184 | tf_op jit(solution)/shard_map/all_to_all | solution.py:67
  927.4 48.6 %concatenate.52 = bf16[2048,2057]{0,1:T(8,128)(2,1)} concatenate(bf16[2048,1]{0,1:T(2,128)(2,1)S(1)} %convert_element_type.617, bf16[2048,512]{0,1:T(8,128)(2,1)} %bitcast.587, bf16[2048,512]{0,1:T(8,128)(2,1)} %bitcast.586, bf16[2048,1024]{0,1:T(8,128)(2,1)} %bitcast.554, bf16[2048,4]{0,1:T(4,128)(2,1)S(1)} %copy-done.129, bf16[2048,4]{0,1:T(4,128)(2,1)S(1)} %copy-done.128), dimensions={1} | concatenate | bytes 16850944 | tf_op jit(solution)/shard_map/concatenate | solution.py:103
  975.9 11.8 copy.788
  1001.1 25.2 %all-to-all-done.1 = bf16[4,128,2048]{2,1,0:T(8,128)(2,1)} async-done(((bf16[4,128,2048]{2,1,0:T(8,128)(2,1)}), bf16[4,128,2048]{2,1,0:T(8,128)(2,1)}, u32[]{:S(2)}, u32[]{:S(2)}) %all-to-all-start.1) | async-done | bytes 2097184 | tf_op jit(solution)/shard_map/all_to_all | solution.py:67
  1049.4 126.1 %all-reduce.43 = (bf16[8,4,128]{0,1,2:T(4,128)(2,1)S(1)}, bf16[4,4,256]{2,1,0:T(4,128)(2,1)S(1)}, bf16[256]{0:T(256)(128)(2,1)S(1)}) all-reduce(bf16[8,4,128]{0,1,2:T(4,128)(2,1)S(1)} %copy.756, ...), channel_id=11, replica_groups=mesh['dp_0'=4,'dp_1'=4,'dp_2'=2,'tensor'=4] {'dp_0','dp_1','dp_2'}, use_global_device_ids=true, to_apply=%region_44.45.clone | all-reduce | flops 8448 | bytes 33792
  1196.6 28.4 %all-gather.32.cloned.1.call-done = bf16[4096,1024]{1,0:T(8,128)(2,1)} async-done(((bf16[128,1024]{1,0:T(8,128)(2,1)}), bf16[4096,1024]{1,0:T(8,128)(2,1)}) %all-gather.32.cloned.1.call-update) | async-done | bytes 8388624 | tf_op jit(solution)/shard_map/all_gather | solution.py:24
  (875 shorter events, 394.1 us)
Async XLA Ops:
  7.2 76.0 %all-gather.22.cloned.1.call-start = ((), (), s32[]{:S(2)}) async-start(), calls=%async_computation.12 | async-start | bytes 9191424 | tf_op jit(solution)/shard_map/all_gather | solution.py:32
  13.6 174.2 %all-gather.20.cloned.1.call-start = ((), (), s32[]{:S(2)}) async-start(), calls=%async_computation.11 | async-start | bytes 34603008 | tf_op jit(solution)/shard_map/all_gather | solution.py:24
  15.9 362.8 %all-gather.24.cloned.1.call-start = ((), (), s32[]{:S(2)}) async-start(), calls=%async_computation.13 | async-start | bytes 4325376 | tf_op jit(solution)/shard_map/all_gather | solution.py:398
  17.6 368.6 %all-gather.34.cloned.1.call-start = ((), (), s32[]{:S(2)}) async-start(), calls=%async_computation.21 | async-start | bytes 4325376 | tf_op jit(solution)/shard_map/all_gather | solution.py:48
  240.6 8.5 collective-permute-start
  297.8 103.0 %all-gather.36.cloned.1.call-start = ((), (), s32[]{:S(2)}) async-start(), calls=%async_computation.22 | async-start | bytes 8650752 | tf_op jit(solution)/shard_map/all_gather | solution.py:48
  301.6 147.9 %all-gather.26.cloned.1.call-start = ((), (), s32[]{:S(2)}) async-start(), calls=%async_computation.14 | async-start | bytes 4325376 | tf_op jit(solution)/shard_map/all_gather | solution.py:399
  303.3 208.9 %all-gather.28.cloned.1.call-start = ((), (), s32[]{:S(2)}) async-start(), calls=%async_computation.15 | async-start | bytes 11894784 | tf_op jit(solution)/shard_map/all_gather | solution.py:32
  307.3 255.0 %all-gather.30.cloned.1.call-start = ((), (), s32[]{:S(2)}) async-start(), calls=%async_computation.16 | async-start | bytes 5947392 | tf_op jit(solution)/shard_map/all_gather | solution.py:406
  454.8 113.4 %all-to-all-start = ((bf16[4,128,2048]{2,1,0:T(8,128)(2,1)}), bf16[4,128,2048]{2,1,0:T(8,128)(2,1)}, u32[]{:S(2)}, u32[]{:S(2)}) async-start(bf16[4,128,2048]{2,1,0:T(8,128)(2,1)} %broadcast_in_dim.100), calls=%async_computation | async-start | bytes 4194304 | tf_op jit(solution)/shard_map/all_to_all | solution.py:67
  602.5 30.9 %all-to-all-start.2 = ((bf16[4,128,2048]{2,1,0:T(8,128)(2,1)}), bf16[4,128,2048]{2,1,0:T(8,128)(2,1)}, u32[]{:S(2)}, u32[]{:S(2)}) async-start(bf16[4,128,2048]{2,1,0:T(8,128)(2,1)} %broadcast_in_dim.102), calls=%async_computation.2 | async-start | bytes 4194304 | tf_op jit(solution)/shard_map/all_to_all | solution.py:67
  607.1 68.9 %all-gather.38.cloned.1.call-start = ((), (), s32[]{:S(2)}) async-start(), calls=%async_computation.23 | async-start | bytes 1310720 | tf_op jit(solution)/shard_map/all_gather | solution.py:86
  654.1 178.3 %all-gather.40.cloned.1.call-start = ((), (), s32[]{:S(2)}) async-start(), calls=%async_computation.24 | async-start | bytes 1310720 | tf_op jit(solution)/shard_map/all_gather | solution.py:86
  683.4 495.5 %reduce-scatter.13.cloned.1.call-start = ((), (), s32[]{:S(2)}) async-start(), calls=%async_computation.19 | async-start | bytes 4325376 | tf_op jit(solution)/shard_map/reduce_scatter | solution.py:663
  689.6 490.9 %reduce-scatter.11.cloned.1.call-start = ((), (), s32[]{:S(2)}) async-start(), calls=%async_computation.18 | async-start | bytes 4325376 | tf_op jit(solution)/shard_map/reduce_scatter | solution.py:655
  695.8 486.4 %reduce-scatter.15.cloned.1.call-start = ((), (), s32[]{:S(2)}) async-start(), calls=%async_computation.20 | async-start | bytes 5947392 | tf_op jit(solution)/shard_map/reduce_scatter | solution.py:684
  701.5 482.5 %reduce-scatter.19.cloned.1.call-start = ((), (), s32[]{:S(2)}) async-start(), calls=%async_computation.26 | async-start | bytes 11894784
  878.3 7.2 collective-permute-start.1
  893.6 30.8 %all-to-all-start.3 = ((bf16[4,128,2048]{2,1,0:T(8,128)(2,1)}), bf16[4,128,2048]{2,1,0:T(8,128)(2,1)}, u32[]{:S(2)}, u32[]{:S(2)}) async-start(bf16[4,128,2048]{2,1,0:T(8,128)(2,1)} %broadcast_in_dim.211), calls=%async_computation.3 | async-start | bytes 4194304 | tf_op jit(solution)/shard_map/all_to_all | solution.py:67
  898.0 290.7 %reduce-scatter.17.cloned.1.call-start = ((), (), s32[]{:S(2)}) async-start(), calls=%async_computation.25 | async-start | bytes 9191424 | tf_op jit(solution)/shard_map/reduce_scatter | solution.py:104
  995.7 30.7 %all-to-all-start.1 = ((bf16[4,128,2048]{2,1,0:T(8,128)(2,1)}), bf16[4,128,2048]{2,1,0:T(8,128)(2,1)}, u32[]{:S(2)}, u32[]{:S(2)}) async-start(bf16[4,128,2048]{2,1,0:T(8,128)(2,1)} %broadcast_in_dim.101), calls=%async_computation.1 | async-start | bytes 4194304 | tf_op jit(solution)/shard_map/all_to_all | solution.py:67
  1000.2 224.8 %all-gather.32.cloned.1.call-start = ((), (), s32[]{:S(2)}) async-start(), calls=%async_computation.17 | async-start | bytes 8650752 | tf_op jit(solution)/shard_map/all_gather | solution.py:24
  1032.4 7.3 all-to-all-start.5
  1040.5 137.7 %all-to-all-start.4 = ((f32[32,1,8]{2,1,0:T(1,128)}), f32[32,1,8]{2,1,0:T(1,128)S(1)}, u32[]{:S(2)}, u32[]{:S(2)}) async-start(f32[32,1,8]{2,1,0:T(1,128)} %broadcast_in_dim.213), calls=%async_computation.4 | async-start | bytes 32768 | tf_op jit(solution)/shard_map/all_to_all | solution.py:67
  (234 other events, 4949.7 us)
Sparse Core Ops, SparseCore 0:
  13.7 58.1 all-gather.21
  74.2 113.5 all-gather.19
  190.7 45.6 all-gather.23
  297.9 47.6 all-gather.33
  348.3 52.4 all-gather.35
  403.6 45.8 all-gather.25
  452.3 59.7 all-gather.27
  514.4 47.8 all-gather.29
  654.2 21.7 all-gather.37
  683.5 23.4 all-gather.39
  710.7 81.6 reduce-scatter.12
  796.3 81.3 reduce-scatter.10
  881.5 84.6 reduce-scatter.14
  970.3 100.9 reduce-scatter.18
  1074.9 93.8 reduce-scatter.16
  1171.2 53.6 all-gather.31
where the time goes:
time: 1260 us; the launch traced here: 1250 us
  waiting for transfers between devices  335 us (27%)
  blocking collectives  270 us (21%)
  local copies, waits for them, and re-layouts  232 us (18%)
  matrix products  232 us (18%)
  other arithmetic  119 us (9%)
  starting transfers between devices  38.6 us (3%)
  between operations  20 us (2%)
    unnamed x2, blocking collectives  188 us
    all_gather x2, waiting for transfers between devices, side_by_side(): lax.all_gather(both, axis, axis=dim, tiled=True)  132 us
    concatenate x2, local copies, waits for them, and re-layouts, in_one_piece(): both = jnp.concatenate(columns, axis=along)  104 us
    all_to_all x6, waiting for transfers between devices, sent_to_all(): lax.all_to_all(jnp.broadcast_to(x[None], (peers, *x.shape)), axis, 0, 0,...  68.7 us
    dot_general x4, matrix products, body(): jnp.einsum('oj,jrd->ord', select, fragment.reshape(blocks, STRETCH, -1),...  53.9 us
    unnamed x496, local copies, waits for them, and re-layouts  53.7 us
    all_gather x2, waiting for transfers between devices, side_by_side_2(): whole = lax.all_gather(both, axis, axis=dim, tiled=True)  52.5 us
    dot_general x10, matrix products, bf_dot(): return jnp.dot(former, latter, preferred_element_type=jnp.float32)  43 us
  transfers between devices with their start and end apart: 24, of which 12 were waited for; matrix products, arithmetic and copies ran while one was open for 40% of the time, Pallas kernels for 0%

commit v1 on v0

v1 whole, which is shorter than its diff:
```python
import functools
import math

import jax
import jax.numpy as jnp
from jax import lax
from jax.experimental import pallas as pl
from jax.experimental.pallas import tpu as pltpu
from jax.sharding import Mesh
from jax.sharding import PartitionSpec as P

MESH = pl.DeviceIdType.MESH
bf16, f32, i32 = jnp.bfloat16, jnp.float32, jnp.int32
HI = lax.Precision.HIGHEST
EPS = 1e-6
STRETCH = 64
D, DK, DV, FFP, HALO = 2048, 128, 256, 384, 16
SEG = 512
ROWS = SEG + HALO
CH = 128
NCH = SEG // CH
NA, NB = 1152, 1152
VLIM = 58 * 1024 * 1024


def at(axis, k):
    n = lax.axis_size(axis)
    return lax.rem(lax.axis_index(axis) + k + n, n)


def greet(peers):
    b = pltpu.get_barrier_semaphore()
    for p in peers:
        pl.semaphore_signal(b, inc=1, device_id=p, device_id_type=MESH)
    pl.semaphore_wait(b, len(peers))


def send(src, dst, ss, rs, who):
    cp = pltpu.make_async_remote_copy(
        src_ref=src, dst_ref=dst, send_sem=ss, recv_sem=rs, device_id=who, device_id_type=MESH
    )
    cp.start()
    return cp


def run(flows):
    flows = list(flows)
    while flows:
        left = []
        for f in flows:
            try:
                next(f)
                left.append(f)
            except StopIteration:
                pass
        flows = left


def peers(**steps):
    return [{ax: at(ax, k)} for ax, ks in steps.items() for k in ks]


def zc_gather(slot, halves, ss, rs):
    z, c = lax.axis_index("z"), lax.axis_index("c")
    other = {"c": 1 - c}
    zp, zm, zf = at("z", 1), at("z", -1), at("z", 2)
    own = slot(z, c)
    a = send(own, own, ss.at[0], rs.at[0], {"z": zp})
    b = send(own, own, ss.at[1], rs.at[1], {"z": zm})
    d0 = send(own, own, ss.at[4], rs.at[4], other)
    yield
    a.wait_recv()
    lo = halves(zm, c)[0]
    e = send(lo, lo, ss.at[2], rs.at[2], {"z": zp})
    m = slot(zm, c)
    d1 = send(m, m, ss.at[5], rs.at[5], other)
    b.wait_recv()
    hi = halves(zp, c)[1]
    f = send(hi, hi, ss.at[3], rs.at[3], {"z": zm})
    p = slot(zp, c)
    d2 = send(p, p, ss.at[6], rs.at[6], other)
    yield
    e.wait_recv()
    fl = halves(zf, c)[0]
    d3 = send(fl, fl, ss.at[7], rs.at[7], other)
    f.wait_recv()
    fh = halves(zf, c)[1]
    d4 = send(fh, fh, ss.at[8], rs.at[8], other)
    yield
    for cp in (d0, d1, d2, d3, d4):
        cp.wait_recv()
    for cp in (a, b, e, f, d0, d1, d2, d3, d4):
        cp.wait_send()


def exchange_flow(src_of, out, ss, rs):
    y, z, c = (lax.axis_index(a) for a in "yzc")
    loc = pltpu.make_async_copy(src_of(y), out.at[y, z, c], ss.at[12])
    loc.start()
    sends = [
        send(src_of(at("y", k)), out.at[y, z, c], ss.at[8 + k], rs.at[8 + k], {"y": at("y", k)})
        for k in (2, 1, 3)
    ]
    yield
    loc.wait()
    for cp in sends:
        cp.wait_recv()
    yield from zc_gather(
        lambda zz, cc: out.at[:, zz, cc],
        lambda zz, cc: (out.at[0:2, zz, cc], out.at[2:4, zz, cc]),
        ss,
        rs,
    )
    for cp in sends:
        cp.wait_send()


def ring_gather(axis, slot, halves, ss, rs):
    i = lax.axis_index(axis)
    p, m = at(axis, 1), at(axis, -1)
    a = send(slot(i), slot(i), ss.at[0], rs.at[0], {axis: p})
    b = send(slot(i), slot(i), ss.at[1], rs.at[1], {axis: m})
    yield
    a.wait_recv()
    lo = halves(m)[0]
    e = send(lo, lo, ss.at[2], rs.at[2], {axis: p})
    b.wait_recv()
    hi = halves(p)[1]
    f = send(hi, hi, ss.at[3], rs.at[3], {axis: m})
    yield
    e.wait_recv()
    f.wait_recv()
    for cp in (a, b, e, f):
        cp.wait_send()


def plane_gather(out, order, lo, mid, hi, ss, rs):
    x, y = lax.axis_index("x"), lax.axis_index("y")
    one, two = slice(lo, hi), (slice(lo, mid), slice(mid, hi))
    if order == "xy":
        yield from ring_gather(
            "x", lambda i: out.at[i, y, one], lambda i: [out.at[i, y, t] for t in two], ss.at[0], rs.at[0]
        )
        yield from ring_gather(
            "y",
            lambda i: out.at[:, i, one],
            lambda i: (out.at[0:2, i, one], out.at[2:4, i, one]),
            ss.at[1],
            rs.at[1],
        )
    else:
        yield from ring_gather(
            "y", lambda i: out.at[x, i, one], lambda i: [out.at[x, i, t] for t in two], ss.at[0], rs.at[0]
        )
        yield from ring_gather(
            "x",
            lambda i: out.at[i, :, one],
            lambda i: (out.at[i, 0:2, one], out.at[i, 2:4, one]),
            ss.at[1],
            rs.at[1],
        )


def ring_scatter(axis, piece, bufs, emit, ss, rs):
    me, p, m, fr = (at(axis, k) for k in (0, 1, -1, 2))
    a = send(piece(fr, 0), bufs.at[0], ss.at[0], rs.at[0], {axis: p})
    c = send(piece(fr, 1), bufs.at[1], ss.at[1], rs.at[1], {axis: m})
    b = send(piece(p, 1), bufs.at[2], ss.at[2], rs.at[2], {axis: p})
    d = send(piece(m, 0), bufs.at[3], ss.at[3], rs.at[3], {axis: m})
    yield
    a.wait_recv()
    bufs[0] = (bufs[0].astype(f32) + piece(p, 0)[...].astype(f32)).astype(bf16)
    e = send(bufs.at[0], bufs.at[4], ss.at[4], rs.at[4], {axis: p})
    c.wait_recv()
    bufs[1] = (bufs[1].astype(f32) + piece(m, 1)[...].astype(f32)).astype(bf16)
    f = send(bufs.at[1], bufs.at[5], ss.at[5], rs.at[5], {axis: m})
    yield
    d.wait_recv()
    e.wait_recv()
    emit(0, piece(me, 0)[...].astype(f32) + bufs[3].astype(f32) + bufs[4].astype(f32))
    b.wait_recv()
    f.wait_recv()
    emit(1, piece(me, 1)[...].astype(f32) + bufs[2].astype(f32) + bufs[5].astype(f32))
    for cp in (a, b, c, d, e, f):
        cp.wait_send()


def plane_scatter(part, res, big, mid, small, h, ss, rs):
    base, q = h * 1024, 512

    def keep(s, v):
        mid[:, :, s * q : (s + 1) * q] = v.astype(bf16)

    def final(s, v):
        res[:, base + s * q : base + (s + 1) * q] = v

    cols = [slice(base + s * q, base + (s + 1) * q) for s in (0, 1)]
    sub = [slice(s * q, (s + 1) * q) for s in (0, 1)]
    if h == 0:
        yield from ring_scatter("x", lambda i, s: part.at[i, :, :, cols[s]], big, keep, ss.at[0], rs.at[0])
        yield from ring_scatter("y", lambda i, s: mid.at[i, :, sub[s]], small, final, ss.at[1], rs.at[1])
    else:
        yield from ring_scatter("y", lambda i, s: part.at[:, i, :, cols[s]], big, keep, ss.at[0], rs.at[0])
        yield from ring_scatter("x", lambda i, s: mid.at[i, :, sub[s]], small, final, ss.at[1], rs.at[1])


SCATTER_SCRATCH = [
    pltpu.VMEM((2, 6, 4, 32, 512), bf16),
    pltpu.VMEM((2, 4, 32, 1024), bf16),
    pltpu.VMEM((2, 6, 32, 512), bf16),
    pltpu.SemaphoreType.DMA((2, 2, 6)),
    pltpu.SemaphoreType.DMA((2, 2, 6)),
]
VM = pl.BlockSpec(memory_space=pltpu.VMEM)
SM = pl.BlockSpec(memory_space=pltpu.SMEM)
HB = pl.BlockSpec(memory_space=pl.ANY)


def shape(dims, kind=f32):
    return jax.ShapeDtypeStruct(dims, kind)


def remote_params(cid):
    return pltpu.CompilerParams(collective_id=cid, has_side_effects=True, vmem_limit_bytes=VLIM)


def exchange(tokens, cotangent, packs, cid):
    n = 2 + len(packs)

    def kernel(*refs):
        ins, outs = refs[:n], refs[n : 2 * n]
        ss, rs = refs[2 * n :]
        x = lax.axis_index("x")
        greet(peers(y=(1, 2, 3), z=(1, 3), c=(1,)))

        def columns(r):
            return lambda yy: r.at[:, pl.ds(pl.multiple_of((x * 4 + yy) * 128, 128), 128)]

        def slots(r):
            return lambda yy: r.at[yy]

        run(
            exchange_flow(columns(ins[i]) if i < 2 else slots(ins[i]), outs[i], ss.at[i], rs.at[i])
            for i in range(n)
        )

    return pl.pallas_call(
        kernel,
        out_shape=[shape((4, 4, 2, 128, 128), bf16)] * 2
        + [shape((4, 4, 2) + p.shape[1:], p.dtype) for p in packs],
        in_specs=[HB] * n,
        out_specs=[HB] * n,
        scratch_shapes=[pltpu.SemaphoreType.DMA((n, 13)), pltpu.SemaphoreType.DMA((n, 12))],
        compiler_params=remote_params(cid),
    )(tokens, cotangent, *packs)


def pick_and_gather(index, tok, cot, cid):
    def kernel(index, tok, cot, xo, do, ss, rs):
        x, y = lax.axis_index("x"), lax.axis_index("y")
        xo[x, y, 0:HALO] = tok[index[0], STRETCH - HALO : STRETCH]
        for j in range(8):
            xo[x, y, HALO + 64 * j : HALO + 64 * (j + 1)] = tok[index[j + 1]]
            do[x, y, 64 * j : 64 * (j + 1)] = cot[index[j + 1]]
        greet(peers(x=(1, 3), y=(1, 3)))
        run(
            [
                plane_gather(xo, "xy", 0, 144, 272, ss.at[0], rs.at[0]),
                plane_gather(xo, "yx", 272, 400, 528, ss.at[1], rs.at[1]),
                plane_gather(do, "xy", 0, 128, 256, ss.at[2], rs.at[2]),
                plane_gather(do, "yx", 256, 384, 512, ss.at[3], rs.at[3]),
            ]
        )

    return pl.pallas_call(
        kernel,
        out_shape=[shape((4, 4, ROWS, 128), bf16), shape((4, 4, SEG, 128), bf16)],
        in_specs=[SM, VM, VM],
        out_specs=[VM, VM],
        scratch_shapes=[pltpu.SemaphoreType.DMA((4, 2, 4)), pltpu.SemaphoreType.DMA((4, 2, 4))],
        compiler_params=remote_params(cid),
    )(index, tok, cot)


def zc_all(a, cid):
    def kernel(a, out, ss, rs):
        z, c = lax.axis_index("z"), lax.axis_index("c")
        out[z, c] = a[...]
        h = a.shape[0] // 2
        greet(peers(z=(1, 3), c=(1,)))
        run(
            [
                zc_gather(
                    lambda zz, cc: out.at[zz, cc],
                    lambda zz, cc: (out.at[zz, cc, 0:h], out.at[zz, cc, h : 2 * h]),
                    ss,
                    rs,
                )
            ]
        )

    return pl.pallas_call(
        kernel,
        out_shape=shape((4, 2) + a.shape, a.dtype),
        in_specs=[VM],
        out_specs=VM,
        scratch_shapes=[pltpu.SemaphoreType.DMA((9,)), pltpu.SemaphoreType.DMA((9,))],
        compiler_params=remote_params(cid),
    )(a)


def gather_rows(out, ss, rs):
    x, y = lax.axis_index("x"), lax.axis_index("y")
    a, b = slice(0, 1024), slice(1024, 2048)
    a2, b2 = (slice(0, 512), slice(512, 1024)), (slice(1024, 1536), slice(1536, 2048))

    def first():
        yield from ring_gather(
            "x", lambda i: out.at[i, y, :, a], lambda i: [out.at[i, y, :, t] for t in a2], ss.at[0, 0], rs.at[0, 0]
        )
        yield from ring_gather(
            "y", lambda i: out.at[:, i, :, a], lambda i: [out.at[:, i, :, t] for t in a2], ss.at[0, 1], rs.at[0, 1]
        )

    def second():
        yield from ring_gather(
            "y", lambda i: out.at[x, i, :, b], lambda i: [out.at[x, i, :, t] for t in b2], ss.at[1, 0], rs.at[1, 0]
        )
        yield from ring_gather(
            "x", lambda i: out.at[i, :, :, b], lambda i: [out.at[i, :, :, t] for t in b2], ss.at[1, 1], rs.at[1, 1]
        )

    return [first(), second()]


def sum_norm_gather(part, xrows, gain, cid):
    def kernel(part, xr, gain, m_out, h_out, acc, big, mid, small, ss, rs, gs, gr):
        x, y = lax.axis_index("x"), lax.axis_index("y")
        greet(peers(x=(1, 3), y=(1, 3)))
        run(
            plane_scatter(part, acc, big.at[h], mid.at[h], small.at[h], h, ss.at[h], rs.at[h]) for h in (0, 1)
        )
        m = xr[...].astype(f32) + acc[...]
        m_out[...] = m
        r = lax.rsqrt(jnp.mean(m * m, axis=-1, keepdims=True) + EPS)
        h_out[x, y] = (m * r * gain[...]).astype(bf16)
        run(gather_rows(h_out, gs, gr))

    return pl.pallas_call(
        kernel,
        out_shape=[shape((32, D)), shape((4, 4, 32, D), bf16)],
        in_specs=[VM] * 3,
        out_specs=[VM] * 2,
        scratch_shapes=[pltpu.VMEM((32, D), f32)]
        + SCATTER_SCRATCH
        + [pltpu.SemaphoreType.DMA((2, 2, 4)), pltpu.SemaphoreType.DMA((2, 2, 4))],
        compiler_params=remote_params(cid),
    )(part, xrows, gain)


def norm_back(v, gain, dh):
    r = lax.rsqrt(jnp.mean(v * v, axis=-1, keepdims=True) + EPS)
    t = gain * dh
    dv = r * t - v * (r * r * r) * jnp.mean(v * t, axis=-1, keepdims=True)
    return dv, jnp.sum(v * r * dh, axis=0, keepdims=True)


def back_middle(part, ypart, m, dyrows, gain, cid):
    def kernel(part, ypart, m, dy, gain, y_out, dm_out, dg_out, da_out, acc, big, mid, small, ss, rs, acc2, big2, mid2, small2, ss2, rs2, gs, gr):
        x, y = lax.axis_index("x"), lax.axis_index("y")
        greet(peers(x=(1, 3), y=(1, 3)))
        run(
            [plane_scatter(part, acc, big.at[h], mid.at[h], small.at[h], h, ss.at[h], rs.at[h]) for h in (0, 1)]
            + [
                plane_scatter(ypart, acc2, big2.at[h], mid2.at[h], small2.at[h], h, ss2.at[h], rs2.at[h])
                for h in (0, 1)
            ]
        )
        mv = m[...]
        dv, dgain = norm_back(mv, gain[...], acc[...])
        dm = dy[...].astype(f32) + dv
        dm_out[...] = dm
        dg_out[...] = dgain
        da_out[x, y] = dm.astype(bf16)
        y_out[...] = (mv + acc2[...]).astype(bf16)
        run(gather_rows(da_out, gs, gr))

    return pl.pallas_call(
        kernel,
        out_shape=[shape((32, D), bf16), shape((32, D)), shape((1, D)), shape((4, 4, 32, D), bf16)],
        in_specs=[VM] * 5,
        out_specs=[VM] * 4,
        scratch_shapes=[pltpu.VMEM((32, D), f32)]
        + SCATTER_SCRATCH
        + [pltpu.VMEM((32, D), f32)]
        + SCATTER_SCRATCH
        + [pltpu.SemaphoreType.DMA((2, 2, 4)), pltpu.SemaphoreType.DMA((2, 2, 4))],
        compiler_params=remote_params(cid),
    )(part, ypart, m, dyrows, gain)


def back_input(part, xrows, dm, gain, cid):
    def kernel(part, xr, dm, gain, dx_out, dg_out, acc, big, mid, small, ss, rs):
        greet(peers(x=(1, 3), y=(1, 3)))
        run(
            plane_scatter(part, acc, big.at[h], mid.at[h], small.at[h], h, ss.at[h], rs.at[h]) for h in (0, 1)
        )
        dv, dgain = norm_back(xr[...].astype(f32), gain[...], acc[...])
        dx_out[...] = (dm[...] + dv).astype(bf16)
        dg_out[...] = dgain

    return pl.pallas_call(
        kernel,
        out_shape=[shape((32, D), bf16), shape((1, D))],
        in_specs=[VM] * 4,
        out_specs=[VM] * 2,
        scratch_shapes=[pltpu.VMEM((32, D), f32)] + SCATTER_SCRATCH,
        compiler_params=remote_params(cid),
    )(part, xrows, dm, gain)


def send_home(order, rows, cid):
    n = len(rows)

    def kernel(order, *refs):
        ins, outs = refs[:n], refs[n : 2 * n]
        gathered = refs[2 * n : 3 * n]
        cols, picks, s1, r1, s2, r2, s3, r3 = refs[3 * n :]
        x, y, z, c = (lax.axis_index(a) for a in "xyzc")
        greet(
            [{"x": at("x", i), "y": at("y", j)} for i in range(4) for j in range(4) if (i, j) != (0, 0)]
            + peers(z=(1, 3), c=(1,))
        )

        def flow(k):
            src, alls = ins[k], gathered[k]
            sends = []
            lane = pl.multiple_of((x * 4 + y) * 128, 128)
            cols[k, x, y] = src[:, pl.ds(lane, 128)]
            t = 0
            for i in range(4):
                for j in range(4):
                    if (i, j) == (0, 0):
                        continue
                    px, py = at("x", i), at("y", j)
                    lane = pl.multiple_of((px * 4 + py) * 128, 128)
                    sends.append(
                        send(src.at[:, pl.ds(lane, 128)], cols.at[k, x, y], s1.at[k, t], r1.at[k, t], {"x": px, "y": py})
                    )
                    t += 1
            yield
            for cp in sends:
                cp.wait_recv()
            alls[z, c] = cols[k].reshape(8, 64, 128)
            yield from zc_gather(
                lambda zz, cc: alls.at[zz, cc],
                lambda zz, cc: (alls.at[zz, cc, 0:4], alls.at[zz, cc, 4:8]),
                s2.at[k],
                r2.at[k],
            )
            for j in range(4):
                for i in range(2):
                    t = j * 2 + i
                    picks[k, j, 64 * i : 64 * (i + 1)] = alls[order[0, t], order[1, t], order[2, t]]
            mine = pl.ds(pl.multiple_of(y * 128, 128), 128)
            last = [
                send(picks.at[k, at("y", j)], outs[k].at[:, mine], s3.at[k, j], r3.at[k, j], {"y": at("y", j)})
                for j in (2, 1, 3)
            ]
            outs[k][:, mine] = picks[k, y]
            yield
            for cp in last:
                cp.wait_recv()
            for cp in sends + last:
                cp.wait_send()

        run(flow(k) for k in range(n))

    return pl.pallas_call(
        kernel,
        out_shape=[shape((128, 512), bf16)] * n,
        in_specs=[SM] + [VM] * n,
        out_specs=[VM] * n,
        scratch_shapes=[pltpu.VMEM((4, 2, 8, 64, 128), bf16)] * n
        + [
            pltpu.VMEM((n, 4, 4, 32, 128), bf16),
            pltpu.VMEM((n, 4, 128, 128), bf16),
            pltpu.SemaphoreType.DMA((n, 15)),
            pltpu.SemaphoreType.DMA((n, 15)),
            pltpu.SemaphoreType.DMA((n, 9)),
            pltpu.SemaphoreType.DMA((n, 9)),
            pltpu.SemaphoreType.DMA((n, 4)),
            pltpu.SemaphoreType.DMA((n, 4)),
        ],
        compiler_params=remote_params(cid),
    )(order, *rows)


def scatter_flow(g, core, bufs, stage, out, ss, rs):
    y, z, c = (lax.axis_index(a) for a in "yzc")
    d = send(g.at[:, :, 1 - c], core, ss.at[0], rs.at[0], {"c": 1 - c})
    yield
    d.wait_recv()

    def add(i, _):
        core[i] = (core[i].astype(f32) + g[i, :, c].astype(f32)).astype(core.dtype)
        return 0

    lax.fori_loop(0, 4, add, 0)

    def emit(s, v):
        stage[2 * s : 2 * s + 2] = v.astype(stage.dtype)

    yield from ring_scatter(
        "z", lambda i, s: core.at[2 * s : 2 * s + 2, i], bufs, emit, ss.at[pl.ds(1, 6)], rs.at[pl.ds(1, 6)]
    )
    sends = [
        send(stage.at[at("y", k)], out.at[y], ss.at[6 + k], rs.at[6 + k], {"y": at("y", k)}) for k in (2, 1, 3)
    ]
    out[y] = stage[y]
    yield
    for cp in sends:
        cp.wait_recv()
    d.wait_send()
    for cp in sends:
        cp.wait_send()


def return_grads(gs, tiny, cid):
    n = len(gs)

    def kernel(*refs):
        ins, outs = refs[: n + 1], refs[n + 1 : 2 * n + 2]
        tot = refs[2 * n + 2]
        rest = refs[2 * n + 3 :]
        cores, bufs, stages = rest[: n + 1], rest[n + 1 : 2 * n + 2], rest[2 * n + 2 : 3 * n + 3]
        xr, ss, rs, xs, xq = rest[3 * n + 3 :]
        x = lax.axis_index("x")
        greet(peers(c=(1,), z=(1, 3), y=(1, 2, 3), x=(1, 2, 3)))

        def last():
            yield from scatter_flow(ins[n], cores[n], bufs[n], stages[n], outs[n], ss.at[n], rs.at[n])
            xr[x] = (outs[n][0].astype(f32) + outs[n][1].astype(f32)) + (outs[n][2].astype(f32) + outs[n][3].astype(f32))
            sends = [send(xr.at[x], xr.at[x], xs.at[k], xq.at[k], {"x": at("x", k)}) for k in (2, 1, 3)]
            yield
            for cp in sends:
                cp.wait_recv()
            tot[...] = (xr[0] + xr[1]) + (xr[2] + xr[3])
            for cp in sends:
                cp.wait_send()

        run(
            [last()]
            + [scatter_flow(ins[i], cores[i], bufs[i], stages[i], outs[i], ss.at[i], rs.at[i]) for i in range(n)]
        )

    arrays = list(gs) + [tiny]
    blocks = [(a.shape[3:], a.dtype) for a in arrays]
    return pl.pallas_call(
        kernel,
        out_shape=[shape((4,) + s, k) for s, k in blocks] + [shape(tiny.shape[3:])],
        in_specs=[VM] * (n + 1),
        out_specs=[VM] * (n + 2),
        scratch_shapes=[pltpu.VMEM((4, 4) + s, k) for s, k in blocks]
        + [pltpu.VMEM((6, 2) + s, k) for s, k in blocks]
        + [pltpu.VMEM((4,) + s, k) for s, k in blocks]
        + [
            pltpu.VMEM((4,) + tiny.shape[3:], f32),
            pltpu.SemaphoreType.DMA((n + 1, 10)),
            pltpu.SemaphoreType.DMA((n + 1, 10)),
            pltpu.SemaphoreType.DMA((4,)),
            pltpu.SemaphoreType.DMA((4,)),
        ],
        compiler_params=remote_params(cid),
    )(*gs, tiny)


def dot(a, b, dims, prec=None):
    return lax.dot_general(a, b, (dims, ((), ())), preferred_element_type=f32, precision=prec)


def lo(a):
    return a.astype(bf16)


def mm(a, b):
    return dot(lo(a), lo(b), ((1,), (0,)))


def mmt(a, b):
    return dot(lo(a), lo(b), ((1,), (1,)))


def tmm(a, b):
    return dot(lo(a), lo(b), ((0,), (0,)))


def halves_of(a):
    h = a.astype(bf16)
    return h, (a - h.astype(f32)).astype(bf16)


def fine(a, b, dims=((1,), (0,))):
    ah, al = halves_of(a)
    bh, bl = halves_of(b)
    return dot(ah, bh, dims) + (dot(ah, bl, dims) + dot(al, bh, dims))


def tri_inverse(a, r, c):
    eye = jnp.where(r == c, 1.0, 0.0)
    n1 = jnp.where((r >> 3) == (c >> 3), -a, 0.0)
    n2 = fine(n1, n1)
    n4 = fine(n2, n2)
    t = eye + n1
    t = t + fine(t, n2)
    t = t + fine(t, n4)
    for level in (3, 4, 5, 6):
        off = ((r >> (level + 1)) == (c >> (level + 1))) & ((r >> level) != (c >> level))
        t = t - fine(t, fine(jnp.where(off, a, 0.0), t))
    return t


def iotas():
    return (
        lax.broadcasted_iota(i32, (CH, CH), 0),
        lax.broadcasted_iota(i32, (CH, CH), 1),
    )


def filtered(z, cw, mc, cols):
    total = z[HALO : HALO + SEG, cols] * cw[3:4, cols]
    for j in range(3):
        total = total + mc[:, j : j + 1] * cw[j : j + 1, cols] * z[HALO - 3 + j : HALO - 3 + j + SEG, cols]
    return total


def silu(v):
    return v * jax.nn.sigmoid(v)


QC, KC, VC = slice(0, 128), slice(128, 256), slice(256, 512)


def decay_of(cc, cr, mask):
    return jnp.exp(jnp.where(mask, cc - cr, 0.0)) * jnp.where(mask, 1.0, 0.0)


def prepare(z, ab, cw, sc, mc, mr):
    def kernel(z, ab, cw, sc, mc, mr, qkv, tm, wu, gb, cr, ti):
        r, c = iotas()
        for cols, scale in ((QC, DK**-0.5), (KC, 1.0)):
            s = silu(filtered(z, cw, mc, cols))
            qkv[:, cols] = (s * lax.rsqrt(jnp.sum(s * s, axis=-1, keepdims=True) + EPS) * scale).astype(bf16)
        qkv[:, VC] = silu(filtered(z, cw, mc, VC)).astype(bf16)
        low = jnp.where(r >= c, 1.0, 0.0)
        eye = jnp.where(r == c, 1.0, 0.0)
        lane = lax.broadcasted_iota(i32, (CH, 128), 1)
        transit = eye
        insert = jnp.zeros((DK, DV), f32)
        for n in range(NCH):
            rows = slice(n * CH, (n + 1) * CH)
            raw = ab[HALO + n * CH : HALO + (n + 1) * CH, :]
            beta = jax.nn.sigmoid(raw[:, 1:2])
            u = raw + sc[0:1, 1:2]
            g = -jnp.exp(sc[0:1, 0:1]) * (jnp.maximum(u, 0.0) + jnp.log1p(jnp.exp(-jnp.abs(u))))
            g = jnp.where(lane == 0, g, 0.0)
            cum = dot(low, g, ((1,), (0,)), HI)[:, 0:1]
            cumr = dot(g, low, ((0,), (1,)), HI)[0:8, :]
            gb[rows, :] = jnp.where(lane == 0, beta, cum)
            cr[:, rows] = cumr
            cumrow = cumr[0:1, :]
            last = cumr[0:1, CH - 1 : CH]
            m = mc[rows, :]
            carried, closing, begin, carry_last = m[:, 3:4], m[:, 4:5], m[:, 5:6], m[0:1, 6:7]
            same = begin == mr[0:1, rows]
            k = qkv[rows, KC]
            kf = k.astype(f32)
            v = qkv[rows, VC].astype(f32)
            a = beta * dot(k, k, ((1,), (1,))) * decay_of(cum, cumrow, same & (r > c))
            t = tri_inverse(a, r, c)
            tm[rows, :] = t
            lead = (beta * jnp.exp(cum) * carried) * kf
            w = fine(t, lead)
            uu = fine(t, beta * v)
            wu[rows, 0:DK] = w
            wu[rows, DK:] = uu
            tail = kf * (jnp.exp(last - cum) * closing)
            keep = jnp.exp(last) * carry_last
            hand = keep * eye - fine(tail, w, ((0,), (0,)))
            insert = fine(hand, insert) + fine(tail, uu, ((0,), (0,)))
            transit = fine(hand, transit)
        ti[:, 0:DK] = transit.astype(bf16)
        ti[:, DK:] = insert.astype(bf16)

    return pl.pallas_call(
        kernel,
        out_shape=[
            shape((SEG, 512), bf16),
            shape((SEG, CH)),
            shape((SEG, DK + DV)),
            shape((SEG, 128)),
            shape((8, SEG)),
            shape((DK, DK + DV), bf16),
        ],
        in_specs=[VM] * 6,
        out_specs=[VM] * 6,
        compiler_params=pltpu.CompilerParams(vmem_limit_bytes=VLIM),
    )(z, ab, cw, sc, mc, mr)


def emit_outputs(where, maps, qkv, wu, gb, cr, mc, mr, gp, hg):
    def kernel(where, maps, qkv, wu, gb, cr, mc, mr, gp, hg, nout, oout, fout, sout):
        r, c = iotas()

        def fold(d, s):
            tr, ins = maps[d, :, 0:DK], maps[d, :, DK:].astype(f32)
            sh, sl = halves_of(s)
            new = dot(tr, sh, ((1,), (0,))) + dot(tr, sl, ((1,), (0,))) + ins
            return jnp.where(d < where[0], new, s)

        s = lax.fori_loop(0, 7, fold, jnp.zeros((DK, DV), f32))
        for n in range(NCH):
            rows = slice(n * CH, (n + 1) * CH)
            m = mc[rows, :]
            carried, closing, begin, carry_last = m[:, 3:4], m[:, 4:5], m[:, 5:6], m[0:1, 6:7]
            cum = gb[rows, 1:2]
            cumrow = cr[0:1, rows]
            last = cr[0:1, n * CH + CH - 1 : n * CH + CH]
            same = begin == mr[0:1, rows]
            q, k = qkv[rows, QC], qkv[rows, KC]
            p = dot(q, k, ((1,), (1,))) * decay_of(cum, cumrow, same & (r >= c))
            fresh = wu[rows, DK:] - fine(wu[rows, 0:DK], s)
            qd = q.astype(f32) * (jnp.exp(cum) * carried)
            o = mm(qd, s) + mm(p, fresh)
            sout[n] = s
            fout[rows, :] = fresh
            oout[rows, :] = o
            x = gp[HALO + n * CH : HALO + (n + 1) * CH, :]
            rn = lax.rsqrt(jnp.mean(o * o, axis=-1, keepdims=True) + EPS)
            nout[rows, :] = (o * rn * hg[0:1, :] * silu(x)).astype(bf16)
            tail = k.astype(f32) * (jnp.exp(last - cum) * closing)
            s = (jnp.exp(last) * carry_last) * s + fine(tail, fresh, ((0,), (0,)))

    return pl.pallas_call(
        kernel,
        out_shape=[shape((SEG, DV), bf16), shape((SEG, DV)), shape((SEG, DV)), shape((NCH, DK, DV))],
        in_specs=[SM] + [VM] * 9,
        out_specs=[VM] * 4,
        compiler_params=pltpu.CompilerParams(vmem_limit_bytes=VLIM),
    )(where, maps, qkv, wu, gb, cr, mc, mr, gp, hg)


def back_emit(dn, o, gp, hg, qkv, wu, gb, cr, mc, mr):
    def kernel(dn, o, gp, hg, qkv, wu, gb, cr, mc, mr, do_out, dgp_out, dhg_out, e_out):
        r, c = iotas()
        dhg = jnp.zeros((1, DV), f32)
        e = jnp.zeros((DK, DV), f32)
        for n in reversed(range(NCH)):
            rows = slice(n * CH, (n + 1) * CH)
            ov, x, dnv = o[rows, :], gp[HALO + n * CH : HALO + (n + 1) * CH, :], dn[rows, :]
            rn = lax.rsqrt(jnp.mean(ov * ov, axis=-1, keepdims=True) + EPS)
            sg = jax.nn.sigmoid(x)
            act = x * sg
            h = hg[0:1, :]
            base = ov * rn
            dhg = dhg + jnp.sum(base * act * dnv, axis=0, keepdims=True)
            dgp_out[rows, :] = (dnv * base * h * (sg * (1.0 + x * (1.0 - sg)))).astype(bf16)
            t = dnv * h * act
            do = rn * t - base * (rn * rn) * jnp.mean(ov * t, axis=-1, keepdims=True)
            do_out[rows, :] = do
            m = mc[rows, :]
            carried, closing, begin, carry_last = m[:, 3:4], m[:, 4:5], m[:, 5:6], m[0:1, 6:7]
            cum = gb[rows, 1:2]
            cumrow = cr[0:1, rows]
            last = cr[0:1, n * CH + CH - 1 : n * CH + CH]
            same = begin == mr[0:1, rows]
            q, k = qkv[rows, QC], qkv[rows, KC]
            p = dot(q, k, ((1,), (1,))) * decay_of(cum, cumrow, same & (r >= c))
            qd = q.astype(f32) * (jnp.exp(cum) * carried)
            tail = k.astype(f32) * (jnp.exp(last - cum) * closing)
            df = tmm(p, do) + mm(tail, e)
            e = tmm(qd, do) + (jnp.exp(last) * carry_last) * e - tmm(wu[rows, 0:DK], df)
        dhg_out[...] = dhg
        e_out[...] = e.astype(bf16)

    return pl.pallas_call(
        kernel,
        out_shape=[shape((SEG, DV)), shape((SEG, DV), bf16), shape((1, DV)), shape((DK, DV), bf16)],
        in_specs=[VM] * 10,
        out_specs=[VM] * 4,
        compiler_params=pltpu.CompilerParams(vmem_limit_bytes=VLIM),
    )(dn, o, gp, hg, qkv, wu, gb, cr, mc, mr)


def back_delta(where, maps, tails, do, fr, st, qkv, tm, wu, gb, cr, z, ab, cw, sc, mc, mr):
    def kernel(
        where, maps, tails, do, fr, st, qkv, tm, wu, gb, cr, z, ab, cw, sc, mc, mr, dz, dab, dcw, dsc, dqkv
    ):
        r, c = iotas()
        low = jnp.where(r >= c, 1.0, 0.0)
        ones = jnp.ones((CH, CH), f32)
        lane = lax.broadcasted_iota(i32, (CH, 128), 1)
        row = lax.broadcasted_iota(i32, (CH, 1), 0)

        def fold(i, e):
            d = 7 - i
            tr, own = maps[d, :, 0:DK], tails[d].astype(f32)
            eh, el = halves_of(e)
            new = dot(tr, eh, ((0,), (0,))) + dot(tr, el, ((0,), (0,))) + own
            return jnp.where(d > where[0], new, e)

        e = lax.fori_loop(0, 7, fold, jnp.zeros((DK, DV), f32))
        acc_a = jnp.zeros((1, 128), f32)
        acc_d = jnp.zeros((1, 128), f32)
        for n in reversed(range(NCH)):
            rows = slice(n * CH, (n + 1) * CH)
            m = mc[rows, :]
            carried, closing, begin, carry_last = m[:, 3:4], m[:, 4:5], m[:, 5:6], m[0:1, 6:7]
            beta, cum = gb[rows, 0:1], gb[rows, 1:2]
            cumrow = cr[0:1, rows]
            last = cr[0:1, n * CH + CH - 1 : n * CH + CH]
            same = begin == mr[0:1, rows]
            q, k = qkv[rows, QC], qkv[rows, KC]
            qf, kf, vf = q.astype(f32), k.astype(f32), qkv[rows, VC].astype(f32)
            dec_i = decay_of(cum, cumrow, same & (r >= c))
            dec_s = jnp.where(r > c, dec_i, 0.0)
            p = dot(q, k, ((1,), (1,))) * dec_i
            kkd = dot(k, k, ((1,), (1,))) * dec_s
            ex = jnp.exp(cum) * carried
            tf = jnp.exp(last - cum) * closing
            keep = jnp.exp(last) * carry_last
            tail = kf * tf
            qd = qf * ex
            dov, fv, sv, tv = do[rows, :], fr[rows, :], st[n], tm[rows, :]
            w, u = wu[rows, 0:DK], wu[rows, DK:]
            df = tmm(p, dov) + mm(tail, e)
            dw = -mmt(df, sv)
            dtail = mmt(fv, e)
            dkeep = jnp.sum(jnp.sum(sv * e, axis=1, keepdims=True), axis=0, keepdims=True)
            dqd = mmt(dov, sv)
            dp = mmt(dov, fv)
            dlead = tmm(tv, dw)
            dbv = tmm(tv, df)
            da = -(mmt(dlead, w) + mmt(dbv, u))
            dakd = da * kkd
            dkk = da * beta * dec_s
            dqk = dp * dec_i
            mix = dakd * beta + dp * p
            dqkv[rows, QC] = mm(dqk, k) + dqd * ex
            dqkv[rows, KC] = (
                tmm(dqk, q) + mm(dkk, k) + tmm(dkk, k) + dlead * (beta * ex) + dtail * tf
            )
            dqkv[rows, VC] = beta * dbv
            lk = jnp.sum(dlead * kf, axis=1, keepdims=True) * ex
            dbeta = jnp.sum(dakd, axis=1, keepdims=True) + lk + jnp.sum(dbv * vf, axis=1, keepdims=True)
            tt = jnp.sum(dtail * tail, axis=1, keepdims=True)
            dcum = jnp.sum(mix, axis=1, keepdims=True) + jnp.sum(dqd * qd, axis=1, keepdims=True) + lk * beta - tt
            dcum = dcum + jnp.where(row == CH - 1, jnp.sum(tt, axis=0, keepdims=True) + dkeep * keep, 0.0)
            full = dcum - dot(mix, ones, ((0,), (0,)), HI)
            dg = dot(low, full, ((0,), (0,)), HI)
            raw = ab[HALO + n * CH : HALO + (n + 1) * CH, :]
            uu = raw + sc[0:1, 1:2]
            rate = -jnp.exp(sc[0:1, 0:1])
            sp = jnp.maximum(uu, 0.0) + jnp.log1p(jnp.exp(-jnp.abs(uu)))
            dal = dg * rate * jax.nn.sigmoid(uu)
            acc_a = acc_a + jnp.sum(dg * rate * sp, axis=0, keepdims=True)
            acc_d = acc_d + jnp.sum(dal, axis=0, keepdims=True)
            dab[rows, :] = jnp.where(
                lane == 0, dal, jnp.where(lane == 1, dbeta * beta * (1.0 - beta), 0.0)
            ).astype(bf16)
            e = tmm(qd, dov) + keep * e - tmm(w, df)
        dsc[0:1, :] = acc_a
        dsc[1:2, :] = acc_d
        dz[0:HALO, :] = jnp.zeros((HALO, 512), f32)
        for cols, scale in ((QC, DK**-0.5), (KC, 1.0), (VC, None)):
            y = filtered(z, cw, mc, cols)
            sg = jax.nn.sigmoid(y)
            ds = dqkv[:, cols]
            if scale is not None:
                s = y * sg
                rn = lax.rsqrt(jnp.sum(s * s, axis=-1, keepdims=True) + EPS)
                ds = scale * (rn * ds - s * (rn * rn * rn) * jnp.sum(s * ds, axis=-1, keepdims=True))
            dy = ds * (sg * (1.0 + y * (1.0 - sg)))
            dz[HALO : HALO + SEG, cols] = dy * cw[3:4, cols]
            dcw[3:4, cols] = jnp.sum(dy * z[HALO : HALO + SEG, cols], axis=0, keepdims=True)
            for j in range(3):
                part = mc[:, j : j + 1] * dy
                away = slice(HALO - 3 + j, HALO - 3 + j + SEG)
                dcw[j : j + 1, cols] = jnp.sum(part * z[away, cols], axis=0, keepdims=True)
                dz[away, cols] = dz[away, cols] + part * cw[j : j + 1, cols]

    return pl.pallas_call(
        kernel,
        out_shape=[shape((ROWS, 512)), shape((SEG, 128), bf16), shape((4, 512)), shape((2, 128))],
        in_specs=[SM] + [VM] * 16,
        out_specs=[VM] * 4,
        scratch_shapes=[pltpu.VMEM((SEG, 512), f32)],
        compiler_params=pltpu.CompilerParams(vmem_limit_bytes=VLIM),
    )(where, maps, tails, do, fr, st, qkv, tm, wu, gb, cr, z, ab, cw, sc, mc, mr)


def wide(a):
    a = jnp.pad(a.astype(bf16), ((0, 0), (0, 4 * FFP - a.shape[1])))
    return a.reshape(a.shape[0], 4, FFP).swapaxes(0, 1)


def body(
    tokens,
    cotangent,
    seq_lengths,
    stretch_order,
    attn_gain,
    w_query,
    w_key,
    w_value,
    w_alpha,
    w_beta,
    conv_query,
    conv_key,
    conv_value,
    a_log,
    dt_bias,
    head_gain,
    w_outgate,
    w_output,
    mlp_gain,
    w_gate,
    w_up,
    w_down,
):
    x, y, z, c = (lax.axis_index(a) for a in "xyzc")
    seg = z * 2 + c
    slot = x * 4 + y
    ff = w_gate.shape[1]

    def by_head(a):
        return a.astype(bf16).swapaxes(0, 1)

    pair = jnp.stack([w_alpha, w_beta], axis=-1).astype(bf16)
    pack_a = jnp.concatenate(
        [
            by_head(w_query),
            by_head(w_key),
            by_head(w_value),
            by_head(w_outgate),
            jnp.pad(pair.swapaxes(0, 1), ((0, 0), (0, 0), (0, 126))),
            w_output.astype(bf16).swapaxes(1, 2),
        ],
        axis=2,
    )
    pack_b = jnp.concatenate([wide(w_gate), wide(w_up), wide(w_down.T)], axis=2)

    def taps(a):
        return a.swapaxes(0, 1).reshape(4, -1)

    def each(a):
        return jnp.broadcast_to(a[None], (4,) + a.shape)

    line = jnp.concatenate(
        [taps(conv_query), taps(conv_key), taps(conv_value), each(head_gain), each(attn_gain), each(mlp_gain)], axis=1
    ).astype(bf16)
    tiny = jnp.broadcast_to(jnp.pad(line, ((0, 0), (0, 256 - line.shape[1])))[:, None], (4, 16, 256))
    tok_all, cot_all, wa, wb, tiny_all = exchange(tokens, cotangent, (pack_a, pack_b, tiny), 1)
    wa = wa.reshape(D, NA)
    wb = wb.reshape(D, NB)
    lines = tiny_all[:, :, :, 0].reshape(32, 256).astype(f32)

    def filters(a):
        return a.reshape(32, 4, -1).swapaxes(0, 1).reshape(4, -1)

    cw = jnp.concatenate([filters(lines[:, 0:16]), filters(lines[:, 16:32]), filters(lines[:, 32:64])], axis=1)
    hg = lines[:, 64:72].reshape(1, DV)
    gain1 = lines[:, 72:136].reshape(1, D)
    gain2 = lines[:, 136:200].reshape(1, D)
    sc = jnp.pad(
        jnp.stack([lax.dynamic_index_in_dim(a_log, y, 0, False), lax.dynamic_index_in_dim(dt_bias, y, 0, False)])[None],
        ((0, 7), (0, 126)),
    )

    blocks = jnp.maximum(seg * 8 - 1 + jnp.arange(9, dtype=i32), 0)
    index = jnp.sum(
        jnp.where(stretch_order[None, :] == blocks[:, None], jnp.arange(64, dtype=i32)[None, :], 0), axis=1, dtype=i32
    )
    xg, dyg = pick_and_gather(index, tok_all.reshape(64, 64, 128), cot_all.reshape(64, 64, 128), 2)
    xs = xg.reshape(16, ROWS, 128).swapaxes(0, 1).reshape(ROWS, D)
    dys = dyg.reshape(16, SEG, 128).swapaxes(0, 1).reshape(SEG, D)
    xrows = lax.dynamic_slice_in_dim(xs, HALO + 32 * slot, 32, 0)
    dyrows = lax.dynamic_slice_in_dim(dys, 32 * slot, 32, 0)

    pos = seg * SEG + jnp.arange(SEG, dtype=i32)
    ends = jnp.cumsum(seq_lengths, dtype=i32)
    begins = ends - seq_lengths
    inside = (pos[:, None] >= begins[None, :]) & (pos[:, None] < ends[None, :])
    begin = jnp.sum(jnp.where(inside, begins[None, :], 0), axis=1, dtype=i32)
    valid = (pos[:, None] - 3 + jnp.arange(3, dtype=i32)[None, :] >= begin[:, None]).astype(f32)
    cb = begin.reshape(NCH, CH)
    first = pos.reshape(NCH, CH)[:, :1]
    carried = (cb < first).astype(f32)
    closing = (cb == cb[:, -1:]).astype(f32)
    carry_last = jnp.broadcast_to(carried[:, -1:], (NCH, CH))
    beginf = begin.astype(f32)
    mc = jnp.concatenate(
        [valid, jnp.stack([carried.reshape(-1), closing.reshape(-1), beginf, carry_last.reshape(-1)], axis=1)], axis=1
    )
    mc = jnp.pad(mc, ((0, 0), (0, 121)))
    mr = jnp.broadcast_to(beginf[None], (8, SEG))
    where = seg.reshape(1).astype(i32)

    xf = xs.astype(f32)
    h1 = (xf * lax.rsqrt(jnp.mean(xf * xf, axis=-1, keepdims=True) + EPS) * gain1).astype(bf16)
    proj = jnp.dot(h1, wa[:, :896], preferred_element_type=f32)
    zq, gp, ab = proj[:, :512], proj[:, 512:768], proj[:, 768:896]
    qkv, tm, wu, gb, cr, ti = prepare(zq, ab, cw, sc, mc, mr)
    maps = zc_all(ti, 3).reshape(8, DK, DK + DV)
    nv, ov, fr, st = emit_outputs(where, maps, qkv, wu, gb, cr, mc, mr, gp, hg)
    wo = wa[:, 896:]
    part = dot(nv, wo, ((1,), (1,))).astype(bf16).reshape(4, 4, 32, D)
    m, h2 = sum_norm_gather(part, xrows, gain2, 4)
    h2 = h2.reshape(SEG, D)
    wg, wu_, wd = wb[:, :FFP], wb[:, FFP : 2 * FFP], wb[:, 2 * FFP :]
    both = jnp.dot(h2, wb[:, : 2 * FFP], preferred_element_type=f32)
    ga, up = both[:, :FFP], both[:, FFP:]
    sg = jax.nn.sigmoid(ga)
    act = ga * sg
    hid = (act * up).astype(bf16)
    ypart = dot(hid, wd, ((1,), (1,))).astype(bf16).reshape(4, 4, 32, D)

    dhid = jnp.dot(dys, wd, preferred_element_type=f32)
    dga = (dhid * up * (sg * (1.0 + ga * (1.0 - sg)))).astype(bf16)
    dup = (dhid * act).astype(bf16)
    dgu = jnp.concatenate([dga, dup], axis=1)
    dh2 = dot(dgu, wb[:, : 2 * FFP], ((1,), (1,))).astype(bf16).reshape(4, 4, 32, D)
    grad_b = jnp.concatenate([dot(h2, dgu, ((0,), (0,))), dot(dys, hid, ((0,), (0,)))], axis=1).astype(bf16)
    yrows, dm, dgain2, da = back_middle(dh2, ypart, m, dyrows, gain2, 5)
    da = da.reshape(SEG, D)
    dn = jnp.dot(da, wo, preferred_element_type=f32)
    do, dgp, dhg, etail = back_emit(dn, ov, gp, hg, qkv, wu, gb, cr, mc, mr)
    tails = zc_all(etail, 6).reshape(8, DK, DV)
    dz, dab, dcw, dsc = back_delta(where, maps, tails, do, fr, st, qkv, tm, wu, gb, cr, zq, ab, cw, sc, mc, mr)
    edge = lax.ppermute(dz[:HALO], ("z", "c"), [(i, i - 1) for i in range(1, 8)])
    dzq = jnp.concatenate([dz[HALO:SEG], dz[SEG:] + edge], axis=0).astype(bf16)
    dproj = jnp.concatenate([dzq, dgp, dab], axis=1)
    dh1 = dot(dproj, wa[:, :896], ((1,), (1,))).astype(bf16).reshape(4, 4, 32, D)
    h1o = h1[HALO:]
    grad_a = jnp.concatenate([dot(h1o, dproj, ((0,), (0,))), dot(da, nv, ((0,), (0,)))], axis=1).astype(bf16)
    dxrows, dgain1 = back_input(dh1, xrows, dm, gain1, 7)
    dp = y * 8 + z * 2 + c
    wanted = stretch_order.reshape(4, 8, 2)
    wanted = lax.dynamic_index_in_dim(wanted, seg, 1, False).reshape(8)
    wanted = jnp.stack([wanted // 16, wanted // 8 % 2, wanted % 8])
    out, dtok = send_home(wanted, (yrows, dxrows), 8)

    def unfilter(a):
        return a.reshape(4, 32, -1).swapaxes(0, 1).reshape(32, -1)

    head = jnp.broadcast_to(dsc[:, 0][None], (32, 2))
    back_line = jnp.concatenate(
        [
            unfilter(dcw[:, QC]),
            unfilter(dcw[:, KC]),
            unfilter(dcw[:, VC]),
            dhg.reshape(32, 8),
            dgain1.reshape(32, 64),
            dgain2.reshape(32, 64),
            head,
        ],
        axis=1,
    )
    back_line = jnp.pad(back_line, ((0, 0), (0, 256 - back_line.shape[1])))
    tiny_back = jnp.pad(back_line[:, None], ((0, 0), (0, 15), (0, 0))).reshape(4, 4, 2, 16, 256).astype(bf16)
    ra, rb, rt, total = return_grads(
        (grad_a.reshape(4, 4, 2, 64, NA), grad_b.reshape(4, 4, 2, 64, NB)), tiny_back, 9
    )
    ra = ra.astype(f32)
    rb = rb.astype(f32)
    rt = rt[:, 0].astype(f32)
    total = total[0]

    def heads(a):
        return a.swapaxes(0, 1)

    def untaps(a):
        return a.reshape(4, 4, -1).swapaxes(0, 1)

    def narrow(a):
        return a.swapaxes(0, 1).reshape(a.shape[1], -1)[:, :ff]

    return (
        out,
        dtok,
        total[72:136],
        heads(ra[:, :, 0:128]),
        heads(ra[:, :, 128:256]),
        heads(ra[:, :, 256:512]),
        heads(ra[:, :, 768]),
        heads(ra[:, :, 769]),
        untaps(rt[:, 0:16]),
        untaps(rt[:, 16:32]),
        untaps(rt[:, 32:64]),
        rt[:, 200],
        rt[:, 201],
        total[64:72],
        heads(ra[:, :, 512:768]),
        ra[:, :, 896:].swapaxes(1, 2),
        total[136:200],
        narrow(rb[:, :, 0:FFP]),
        narrow(rb[:, :, FFP : 2 * FFP]),
        narrow(rb[:, :, 2 * FFP :]).T,
    )


def solution(mesh):
    torus = Mesh(mesh.devices.reshape(4, 4, 2, 4), ("y", "z", "c", "x"))
    dp, tp = ("y", "z", "c"), "x"
    in_specs = (
        P(dp, None),
        P(dp, None),
        P(),
        P(),
        P(dp),
        P(dp, tp, None),
        P(dp, tp, None),
        P(dp, tp, None),
        P(dp, tp),
        P(dp, tp),
        P(None, tp, dp),
        P(None, tp, dp),
        P(None, tp, dp),
        P(tp),
        P(tp),
        P(dp),
        P(dp, tp, None),
        P(tp, None, dp),
        P(dp),
        P(dp, tp),
        P(dp, tp),
        P(tp, dp),
    )
    out_specs = (
        P(dp, tp),
        P(dp, tp),
        P(dp),
        P(dp, tp, None),
        P(dp, tp, None),
        P(dp, tp, None),
        P(dp, tp),
        P(dp, tp),
        P(None, tp, dp),
        P(None, tp, dp),
        P(None, tp, dp),
        P(tp),
        P(tp),
        P(dp),
        P(dp, tp, None),
        P(tp, None, dp),
        P(dp),
        P(dp, tp),
        P(dp, tp),
        P(tp, dp),
    )
    return jax.shard_map(body, mesh=torus, in_specs=in_specs, out_specs=out_specs, check_vma=False)
```

time: 1260 us -> 500 us (0.40)
  Pallas kernels: 0 us -> 376 us
  waiting for transfers between devices: 335 us -> 0.01 us
  blocking collectives: 270 us -> 0 us
  local copies, waits for them, and re-layouts: 232 us -> 44.5 us
  matrix products: 232 us -> 44.7 us
  other arithmetic: 119 us -> 26.2 us
  starting transfers between devices: 38.6 us -> 2.05 us
  between operations: 20 us -> 1.74 us
    pallas_call x0 -> x13, Pallas kernels: none -> 376 us  [the longest x1 65.2 us: exchange(): pl.pallas_call(kernel, out_shape=[shape((4, 4, 2, 128, 128), bf16)] * 2 +...]
    all_gather x11 -> x0, waiting for transfers between devices: 265 us -> none  [the longest x2 132 us: side_by_side(): lax.all_gather(both, axis, axis=dim, tiled=True)]
    unnamed x2 -> x0, blocking collectives: 188 us -> none
    dot_general x98 -> x12, matrix products: 230 us -> 44.7 us  [the longest x8 29.2 us: dot(): lax.dot_general(a, b, (dims, ((), ())), preferred_element_type=f32, preci...]
    concatenate x5, local copies, waits for them, and re-layouts: 107 us -> 0.38 us  [the longest x2 0.18 us: body(): jnp.concatenate([valid, jnp.stack([carried.reshape(-1), closing.reshape(-...]
    all_gather x6 -> x0, blocking collectives: 81.6 us -> none  [the longest x4 30 us: entering(): lax.all_gather(part.astype(kind), axis)]
    all_to_all x6 -> x0, waiting for transfers between devices: 68.7 us -> none  [sent_to_all(): lax.all_to_all(jnp.broadcast_to(x[None], (peers, *x.shape)), axis, 0, 0,...]
    unnamed x496 -> x90, local copies, waits for them, and re-layouts: 53.7 us -> 10.3 us
  transfers between devices with their start and end apart: 24 -> 1, of which waited for: 12 -> 0; matrix products, arithmetic and copies ran while one was open for 40% -> 4% of each run, Pallas kernels for 0% -> 0%
where the time goes in v1:
time: 500 us; the launch traced here: 496 us
  Pallas kernels  376 us (75%)
  matrix products  44.7 us (9%)
  local copies, waits for them, and re-layouts  44.5 us (9%)
  other arithmetic  26.2 us (5%)
    pallas_call x1, Pallas kernels, exchange(): pl.pallas_call(kernel, out_shape=[shape((4, 4, 2, 128, 128), bf16)] * 2 +...  65.2 us
    pallas_call x1, Pallas kernels, return_grads(): pl.pallas_call(kernel, out_shape=[shape((4,) + s, k) for s, k in blocks]...  62.3 us
    pallas_call x1, Pallas kernels, back_middle(): pl.pallas_call(kernel, out_shape=[shape((32, D), bf16), shape((32, D)), s...  43.7 us
    pallas_call x1, Pallas kernels, sum_norm_gather(): pl.pallas_call(kernel, out_shape=[shape((32, D)), shape((4, 4, 32, D), bf...  38.4 us
    pallas_call x2, Pallas kernels, zc_all(): pl.pallas_call(kernel, out_shape=shape((4, 2) + a.shape, a.dtype), in_spe...  37.2 us
    pallas_call x1, Pallas kernels, pick_and_gather(): pl.pallas_call(kernel, out_shape=[shape((4, 4, ROWS, 128), bf16), shape((...  31 us
    dot_general x8, matrix products, dot(): lax.dot_general(a, b, (dims, ((), ())), preferred_element_type=f32, preci...  29.2 us
    pallas_call x1, Pallas kernels, send_home(): pl.pallas_call(kernel, out_shape=[shape((128, 512), bf16)] * n, in_specs=...  29 us
  transfers between devices with their start and end apart: 1, of which 0 were waited for; matrix products, arithmetic and copies ran while one was open for 4% of the time, Pallas kernels for 0%

profile of v1, /device:TPU:1, one launch (start us, length us, event | category | flops | bytes accessed | tf_op | source)
XLA Modules:
  0.0 495.5 jit_solution(7361880275963381572)
XLA Ops:
  10.3 65.2 %shard_map.365 = (bf16[4,4,2,128,128]{4,3,2,1,0:T(8,128)(2,1)}, bf16[4,4,2,128,128]{4,3,2,1,0:T(8,128)(2,1)}, bf16[4,4,2,64,1152]{4,3,2,1,0:T(8,128)(2,1)}, bf16...) custom-call(bf16[128,2048]{1,0:T(8,128)(2,1)} %refs_0_.1, bf16[128,2048]{1,0:T(8,128)(2,1)} %refs_1_.1, ...), custom_call_target="tpu_custom_call" | custom-call | tf_op jit(solution)/shard_map/pallas_call | solution.py:247
  77.6 31.0 %shard_map.366 = (bf16[4,4,528,128]{3,2,1,0:T(8,128)(2,1)}, bf16[4,4,512,128]{3,2,1,0:T(8,128)(2,1)}) custom-call(s32[9]{0:T(128)} %select_reduce_fusion.1.index, bf16[64,64,128]{2,1,0:T(8,128)(2,1)} %bitcast.208, bf16[64,64,128]{2,1,0:T(8,128)(2,1)} %bitcast.209), custom_call_target="tpu_custom_call" | custom-call | tf_op jit(solution)/shard_map/pallas_call | solution.py:275
  108.6 3.1 multiply_reduce_fusion
  115.0 5.2 %fusion.2 = f32[528,896]{1,0:T(8,128)S(1)} fusion(bf16[528,2048]{1,0:T(8,128)(2,1)S(1)} %multiply_convert_fusion, bf16[2048,1152]{1,0:T(8,128)(2,1)} %bitcast.216), kind=kOutput, calls=%fused_computation.7 | convolution fusion | flops 1937768448 | bytes 7725056 | tf_op jit(solution)/shard_map/dot_general | solution.py:1011
  133.5 25.2 %shard_map.367 = (bf16[512,512]{1,0:T(8,128)(2,1)}, f32[512,128]{1,0:T(8,128)}, f32[512,384]{1,0:T(8,128)}, f32[512,128]{1,0:T(8,128)}, f32[8,512]{1,0:T(8,128)}, /*index=5*/bf16[128,384]{1,0:T(8,128)(2,1)}) custom-call(f32[528,512]{1,0:T(8,128)} %slice.222.z, f32[528,128]{1,0:T(8,128)} %slice.223.ab, f32[4,512]{1,0:T(4,128)} %copy-done.19, ...), custom_call_target="tpu_custom_call" | custom-call | tf_op jit(solution)/shard_map/pallas_call | solution.py:695
  158.7 14.8 %shard_map.368 = bf16[4,2,128,384]{3,2,1,0:T(8,128)(2,1)} custom-call(bf16[128,384]{1,0:T(8,128)(2,1)} %get-tuple-element.66.a), custom_call_target="tpu_custom_call" | custom-call | tf_op jit(solution)/shard_map/pallas_call | solution.py:302
  173.5 6.0 %shard_map.369 = (bf16[512,256]{1,0:T(8,128)(2,1)}, f32[512,256]{1,0:T(8,128)}, f32[512,256]{1,0:T(8,128)}, f32[4,128,256]{2,1,0:T(8,128)}) custom-call(s32[1]{0:T(128)} %bitcast.20.where, bf16[8,128,384]{2,1,0:T(8,128)(2,1)} %bitcast.190, bf16[512,512]{1,0:T(8,128)(2,1)} %get-tuple-element.67.qkv, f32[512,384]{1,0:T(8,128)} %get-tuple-element.68.wu, ...), custom_call_target="tpu_custom_call" | custom-call | tf_op jit(solution)/shard_map/pallas_call | solution.py:744
  179.6 3.4 convolution_convert_fusion.1
  184.5 38.4 %shard_map.370 = (f32[32,2048]{1,0:T(8,128)}, bf16[4,4,32,2048]{3,2,1,0:T(8,128)(2,1)}) custom-call(bf16[4,4,32,2048]{3,2,1,0:T(8,128)(2,1)} %bitcast.188, bf16[32,2048]{1,0:T(8,128)(2,1)} %constant_dynamic-slice_fusion.1.xr, f32[1,2048]{1,0:T(1,128)} %reshape.532.gain), custom_call_target="tpu_custom_call" | custom-call | tf_op jit(solution)/shard_map/pallas_call | solution.py:349
  223.0 4.5 fusion.8
  232.9 5.2 %convolution_convert_fusion.3 = bf16[512,2048]{1,0:T(8,128)(2,1)} fusion(bf16[2048,1152]{1,0:T(8,128)(2,1)} %bitcast.245, bf16[512,384]{0,1:T(8,128)(2,1)} %get-tuple-element.203, bf16[512,384]{0,1:T(8,128)(2,1)S(1)} %get-tuple-element.202), kind=kOutput, calls=%fused_computation.12 | convolution fusion | flops 1613234176 | bytes 6029312 | tf_op jit(solution)/shard_map/dot_general | solution.py:579
  238.1 43.7 %shard_map.371 = (bf16[32,2048]{1,0:T(8,128)(2,1)}, f32[32,2048]{1,0:T(8,128)}, f32[1,2048]{1,0:T(1,128)}, bf16[4,4,32,2048]{3,2,1,0:T(8,128)(2,1)}) custom-call(bf16[4,4,32,2048]{3,2,1,0:T(8,128)(2,1)} %bitcast.202, bf16[4,4,32,2048]{3,2,1,0:T(8,128)(2,1)} %bitcast.201, f32[32,2048]{1,0:T(8,128)} %get-tuple-element.73.m, ...), custom_call_target="tpu_custom_call" | custom-call | tf_op jit(solution)/shard_map/pallas_call | solution.py:388
  281.8 3.8 fusion.14.dn
  285.6 4.7 shard_map.372
  290.3 22.4 %shard_map.373 = bf16[4,2,128,256]{3,2,1,0:T(8,128)(2,1)} custom-call(bf16[128,256]{1,0:T(8,128)(2,1)} %get-tuple-element.77.a), custom_call_target="tpu_custom_call" | custom-call | tf_op jit(solution)/shard_map/pallas_call | solution.py:302
  312.7 12.1 %shard_map.374 = (f32[528,512]{1,0:T(8,128)}, bf16[512,128]{1,0:T(8,128)(2,1)}, f32[4,512]{1,0:T(4,128)}, f32[2,128]{1,0:T(2,128)}) custom-call(s32[1]{0:T(128)} %bitcast.20.where, bf16[8,128,384]{2,1,0:T(8,128)(2,1)} %bitcast.191, bf16[8,128,256]{2,1,0:T(8,128)(2,1)} %bitcast.194, f32[512,256]{1,0:T(8,128)} %get-tuple-element.78.do, ...), custom_call_target="tpu_custom_call" | custom-call | tf_op jit(solution)/shard_map/pallas_call | solution.py:892
  330.7 4.1 convolution_convert_fusion.5
  341.5 3.1 convolution_convert_fusion.4
  349.9 5.9 %fusion.4 = bf16[512,2048]{1,0:T(8,128)(2,1)} fusion(bf16[2048,1152]{1,0:T(8,128)(2,1)} %bitcast.219, bf16[512,128]{1,0:T(8,128)(2,1)S(1)} %copy-done.24, bf16[512,256]{1,0:T(8,128)(2,1)S(1)} %copy-done.23, bf16[16,512]{1,0:T(8,128)(2,1)S(1)} %add_convert_fusion, bf16[496,512]{1,0:T(8,128)(2,1)S(1)} %slice.310), kind=kOutput, calls=%fused_computation.9 | convolution fusion | flops 1883766784 | bytes 6684672 | tf_op jit(solution)/shard_map/dot_general | solution.py:579
  355.8 4.2 convolution_convert_fusion
  360.0 21.4 %shard_map.375 = (bf16[32,2048]{1,0:T(8,128)(2,1)}, f32[1,2048]{1,0:T(1,128)}) custom-call(bf16[4,4,32,2048]{3,2,1,0:T(8,128)(2,1)} %bitcast.195, bf16[32,2048]{1,0:T(8,128)(2,1)} %constant_dynamic-slice_fusion.1.xr, f32[32,2048]{1,0:T(8,128)} %get-tuple-element.85.dm, f32[1,2048]{1,0:T(1,128)} %reshape.539.gain), custom_call_target="tpu_custom_call" | custom-call | tf_op jit(solution)/shard_map/pallas_call | solution.py:412
  383.1 4.7 pad_maximum_fusion.refs_0_
  387.8 62.3 %shard_map.377 = (bf16[4,64,1152]{2,1,0:T(8,128)(2,1)}, bf16[4,64,1152]{2,1,0:T(8,128)(2,1)}, bf16[4,16,256]{2,1,0:T(8,128)(2,1)}, f32[16,256]{1,0:T(8,128)}) custom-call(bf16[4,4,2,64,1152]{4,3,2,1,0:T(8,128)(2,1)} %pad_maximum_fusion.refs_0_, bf16[4,4,2,64,1152]{4,3,2,1,0:T(8,128)(2,1)} %pad_maximum_fusion.1.refs_1_, bf16[4,4,2,16,256]{4,3,2,1,0:T(8,128)(2,1)} %bitcast.210), custom_call_target="tpu_custom_call" | custom-call | tf_op jit(solution)/shard_map/pallas_call | solution.py:559
  457.1 29.0 %shard_map.376 = (bf16[128,512]{1,0:T(8,128)(2,1)}, bf16[128,512]{1,0:T(8,128)(2,1)}) custom-call(s32[3,8]{1,0:T(4,128)} %pad_add_fusion.order, bf16[32,2048]{1,0:T(8,128)(2,1)} %get-tuple-element.74.refs_0_, bf16[32,2048]{1,0:T(8,128)(2,1)} %get-tuple-element.86.refs_1_), custom_call_target="tpu_custom_call" | custom-call | tf_op jit(solution)/shard_map/pallas_call | solution.py:479
  (233 shorter events, 70.3 us)
Async XLA Ops:
  0.7 7.7 %copy-start.10 = (f32[1376,64]{0,1:T(8,128)S(1)}, f32[1376,64]{0,1:T(8,128)}, u32[]{:S(2)}) copy-start(f32[1376,64]{0,1:T(8,128)} %param.43) | copy-start | bytes 1056772
  0.7 7.7 %copy-start.15 = (f32[64,4,128]{2,1,0:T(4,128)S(1)}, f32[64,4,128]{2,1,0:T(4,128)}, u32[]{:S(2)}) copy-start(f32[64,4,128]{2,1,0:T(4,128)} %param.27) | copy-start | bytes 393220
  8.7 68.2 %copy-start.22 = (s32[64]{0:T(128)S(1)}, s32[64]{0:T(128)}, u32[]{:S(2)}) copy-start(s32[64]{0:T(128)} %param.25) | copy-start | bytes 772
  108.6 3.1 copy-start
  115.0 5.2 %copy-start.3 = (bf16[528,2048]{1,0:T(8,128)(2,1)}, bf16[528,2048]{1,0:T(8,128)(2,1)S(1)}, u32[]{:S(2)}) copy-start(bf16[528,2048]{1,0:T(8,128)(2,1)S(1)} %multiply_convert_fusion) | copy-start | bytes 6488068
  120.3 3.3 copy-start.28
  120.3 3.9 copy-start.29
  121.9 8.3 %copy-start.5 = (bf16[4,4,512,128]{3,2,1,0:T(8,128)(2,1)S(1)}, bf16[4,4,512,128]{3,2,1,0:T(8,128)(2,1)}, u32[]{:S(2)}) copy-start(bf16[4,4,512,128]{3,2,1,0:T(8,128)(2,1)} %get-tuple-element.61) | copy-start | bytes 6291460
  184.5 43.0 %slice-start = ((s8[4718592]{0:T(1024)(128)(4,1)}), s8[524288]{0:T(1024)(128)(4,1)S(1)}, s32[]{:S(2)}) async-start(s8[4718592]{0:T(1024)(128)(4,1)} %bitcast.246), calls=%async_computation | async-start | bytes 1048576
  223.0 4.5 copy-start.2
  223.0 4.5 slice-start.1
  229.6 3.3 copy-start.30
  325.6 24.2 %collective-permute-start = (f32[16,512]{1,0:T(8,128)S(1)}, f32[16,512]{1,0:T(8,128)S(1)}, u32[]{:S(2)}, u32[]{:S(2)}) collective-permute-start(f32[16,512]{1,0:T(8,128)S(1)} %slice.188), channel_id=1, source_target_pairs={{4,0},{8,4},{12,8},{16,12},{20,16},{24,20},{28,24},{5,1},{9,5},{13... | collective-permute-start | bytes 98312 | tf_op jit(solution)/shard_map/ppermute | solution.py:1040
  330.6 4.1 copy-start.20
  330.6 4.1 copy-start.25
  330.7 4.2 copy-start.21
  330.7 4.2 copy-start.26
  341.5 3.1 copy-start.6
  344.6 4.1 copy-start.11
  344.6 5.3 %copy-start.23 = (bf16[512,256]{1,0:T(8,128)(2,1)S(1)}, bf16[512,256]{1,0:T(8,128)(2,1)}, u32[]{:S(2)}) copy-start(bf16[512,256]{1,0:T(8,128)(2,1)} %get-tuple-element.83) | copy-start | bytes 786436
  344.6 5.3 %copy-start.24 = (bf16[512,128]{1,0:T(8,128)(2,1)S(1)}, bf16[512,128]{1,0:T(8,128)(2,1)}, u32[]{:S(2)}) copy-start(bf16[512,128]{1,0:T(8,128)(2,1)} %get-tuple-element.84) | copy-start | bytes 393220
  349.9 5.9 %copy-start.4 = (bf16[528,2048]{1,0:T(8,128)(2,1)S(1)}, bf16[528,2048]{1,0:T(8,128)(2,1)}, u32[]{:S(2)}) copy-start(bf16[528,2048]{1,0:T(8,128)(2,1)} %copy-done.3) | copy-start | bytes 6488068
  455.5 35.9 %copy-start.9 = (bf16[4,64,1152]{2,1,0:T(8,128)(2,1)S(1)}, bf16[4,64,1152]{2,1,0:T(8,128)(2,1)}, u32[]{:S(2)}) copy-start(bf16[4,64,1152]{2,1,0:T(8,128)(2,1)} %get-tuple-element.97) | copy-start | bytes 1769476
  491.6 3.0 copy-start.17
  (10 other events, 19.8 us)

commit v2 on v1

v2 whole, which is shorter than its diff:
```python
import functools
import math

import jax
import jax.numpy as jnp
from jax import lax
from jax.experimental import pallas as pl
from jax.experimental.pallas import tpu as pltpu
from jax.sharding import Mesh
from jax.sharding import PartitionSpec as P

MESH = pl.DeviceIdType.MESH
bf16, f32, i32 = jnp.bfloat16, jnp.float32, jnp.int32
HI = lax.Precision.HIGHEST
EPS = 1e-6
STRETCH = 64
D, DK, DV, FFP, HALO = 2048, 128, 256, 384, 16
SEG = 512
ROWS = SEG + HALO
CH = 128
NCH = SEG // CH
NA, NB = 1152, 1152
VLIM = 58 * 1024 * 1024


def at(axis, k):
    n = lax.axis_size(axis)
    return lax.rem(lax.axis_index(axis) + k + n, n)


def greet(peers):
    b = pltpu.get_barrier_semaphore()
    for p in peers:
        pl.semaphore_signal(b, inc=1, device_id=p, device_id_type=MESH)
    pl.semaphore_wait(b, len(peers))


def send(src, dst, ss, rs, who):
    cp = pltpu.make_async_remote_copy(
        src_ref=src, dst_ref=dst, send_sem=ss, recv_sem=rs, device_id=who, device_id_type=MESH
    )
    cp.start()
    return cp


def run(flows, plan=""):
    flows = list(flows)
    for i in plan:
        next(flows[int(i)], None)
    for _ in together(flows):
        pass


def together(flows):
    flows = list(flows)
    while flows:
        left = []
        for f in flows:
            try:
                next(f)
                left.append(f)
            except StopIteration:
                pass
        flows = left
        if flows:
            yield


def segment_peers():
    z, c = lax.axis_index("z"), lax.axis_index("c")
    out = []
    for k in range(4):
        for d in range(2):
            if (k, d) != (0, 0):
                out.append({"z": at("z", k), "c": lax.rem(c + d, 2)})
    return out


def plane_peers():
    return [{"x": at("x", i), "y": at("y", j)} for i in range(4) for j in range(4) if (i, j) != (0, 0)]


def peers(**steps):
    return [{ax: at(ax, k)} for ax, ks in steps.items() for k in ks]


def zc_gather(slot, halves, ss, rs):
    z, c = lax.axis_index("z"), lax.axis_index("c")
    other = {"c": 1 - c}
    zp, zm, zf = at("z", 1), at("z", -1), at("z", 2)
    own, (o1, o2) = slot(z, c), halves(z, c)
    a = send(o1, o1, ss.at[0], rs.at[0], {"z": zp})
    b = send(o2, o2, ss.at[1], rs.at[1], {"z": zm})
    a2 = send(o2, o2, ss.at[9], rs.at[9], {"z": zp})
    b2 = send(o1, o1, ss.at[10], rs.at[10], {"z": zm})
    d0 = send(own, own, ss.at[4], rs.at[4], other)
    yield
    a.wait_recv()
    lo = halves(zm, c)[0]
    e = send(lo, lo, ss.at[2], rs.at[2], {"z": zp})
    b.wait_recv()
    hi = halves(zp, c)[1]
    f = send(hi, hi, ss.at[3], rs.at[3], {"z": zm})
    yield
    a2.wait_recv()
    m = slot(zm, c)
    d1 = send(m, m, ss.at[5], rs.at[5], other)
    b2.wait_recv()
    p = slot(zp, c)
    d2 = send(p, p, ss.at[6], rs.at[6], other)
    yield
    e.wait_recv()
    fl = halves(zf, c)[0]
    d3 = send(fl, fl, ss.at[7], rs.at[7], other)
    f.wait_recv()
    fh = halves(zf, c)[1]
    d4 = send(fh, fh, ss.at[8], rs.at[8], other)
    yield
    for cp in (d0, d1, d2, d3, d4):
        cp.wait_recv()
    for cp in (a, b, a2, b2, e, f, d0, d1, d2, d3, d4):
        cp.wait_send()


def trade_flow(src_of, dst, ss, rs):
    y = lax.axis_index("y")
    loc = pltpu.make_async_copy(src_of(y), dst(y), ss.at[3])
    loc.start()
    sends = [
        send(src_of(at("y", k)), dst(y), ss.at[k - 1], rs.at[k - 1], {"y": at("y", k)}) for k in (2, 1, 3)
    ]
    yield
    loc.wait()
    for cp in sends:
        cp.wait_recv()
    for cp in sends:
        cp.wait_send()


def spread_flow(out, ss, rs):
    return zc_gather(
        lambda zz, cc: out.at[:, zz, cc],
        lambda zz, cc: (out.at[0:2, zz, cc], out.at[2:4, zz, cc]),
        ss,
        rs,
    )


def exchange_flow(src_of, out, ss, rs):
    z, c = lax.axis_index("z"), lax.axis_index("c")
    yield from trade_flow(src_of, lambda y: out.at[y, z, c], ss.at[pl.ds(11, 4)], rs.at[pl.ds(11, 4)])
    yield from spread_flow(out, ss, rs)


def torus_gather(a1, a2, block, ss, rs):
    i, j = lax.axis_index(a1), lax.axis_index(a2)
    p1, m1, f1 = (at(a1, k) for k in (1, -1, 2))
    p2, m2 = at(a2, 1), at(a2, -1)
    all_of = []

    def go(ref, who):
        k = len(all_of)
        all_of.append(send(ref, ref, ss.at[k], rs.at[k], who))
        return all_of[-1]

    def along(i1):
        b = block(i1, j, None)
        return go(b, {a2: p2}), go(b, {a2: m2})

    def forward(i1, pair):
        pair[0].wait_recv()
        go(block(i1, m2, 0), {a2: p2})
        pair[1].wait_recv()
        go(block(i1, p2, 1), {a2: m2})

    own = block(i, j, None)
    a, b = go(own, {a1: p1}), go(own, {a1: m1})
    s0 = along(i)
    yield
    a.wait_recv()
    e = go(block(m1, j, 0), {a1: p1})
    b.wait_recv()
    f = go(block(p1, j, 1), {a1: m1})
    s1 = along(m1)
    s2 = along(p1)
    yield
    forward(i, s0)
    yield
    e.wait_recv()
    f.wait_recv()
    s3 = along(f1)
    yield
    forward(m1, s1)
    forward(p1, s2)
    yield
    forward(f1, s3)
    yield
    done = [a, b, e, f] + [cp for pair in (s0, s1, s2, s3) for cp in pair]
    for cp in all_of:
        if not any(cp is d for d in done):
            cp.wait_recv()
    for cp in all_of:
        cp.wait_send()


def lanes(i, j):
    return pl.ds(pl.multiple_of((i * 4 + j) * 128, 128), 128)


def gather_columns(out, skip, ss, rs):
    def half(lo, mid, hi):
        rows = {None: slice(lo, hi), 0: slice(lo, mid), 1: slice(mid, hi)}
        return lambda x, y, part: out.at[rows[part], lanes(x, y)]

    one, two = half(0, skip + 128, skip + 256), half(skip + 256, skip + 384, skip + 512)
    yield from together(
        [
            torus_gather("x", "y", one, ss.at[0], rs.at[0]),
            torus_gather("y", "x", lambda y, x, part: two(x, y, part), ss.at[1], rs.at[1]),
        ]
    )


def gather_rows(out, ss, rs):
    def half(lo):
        cols = {None: slice(lo, lo + 1024), 0: slice(lo, lo + 512), 1: slice(lo + 512, lo + 1024)}
        return lambda x, y, part: out.at[x, y, :, cols[part]]

    one, two = half(0), half(1024)
    yield from together(
        [
            torus_gather("x", "y", one, ss.at[0], rs.at[0]),
            torus_gather("y", "x", lambda y, x, part: two(x, y, part), ss.at[1], rs.at[1]),
        ]
    )


GATHER_SEMS = [pltpu.SemaphoreType.DMA((2, 20)), pltpu.SemaphoreType.DMA((2, 20))]


def ring_scatter(axis, piece, bufs, emit, ss, rs):
    me, p, m, fr = (at(axis, k) for k in (0, 1, -1, 2))
    a = send(piece(fr, 0), bufs.at[0], ss.at[0], rs.at[0], {axis: p})
    c = send(piece(fr, 1), bufs.at[1], ss.at[1], rs.at[1], {axis: m})
    b = send(piece(p, 1), bufs.at[2], ss.at[2], rs.at[2], {axis: p})
    d = send(piece(m, 0), bufs.at[3], ss.at[3], rs.at[3], {axis: m})
    yield
    a.wait_recv()
    bufs[0] = (bufs[0].astype(f32) + piece(p, 0)[...].astype(f32)).astype(bufs.dtype)
    e = send(bufs.at[0], bufs.at[4], ss.at[4], rs.at[4], {axis: p})
    c.wait_recv()
    bufs[1] = (bufs[1].astype(f32) + piece(m, 1)[...].astype(f32)).astype(bufs.dtype)
    f = send(bufs.at[1], bufs.at[5], ss.at[5], rs.at[5], {axis: m})
    yield
    d.wait_recv()
    e.wait_recv()
    emit(0, piece(me, 0)[...].astype(f32) + bufs[3].astype(f32) + bufs[4].astype(f32))
    b.wait_recv()
    f.wait_recv()
    emit(1, piece(me, 1)[...].astype(f32) + bufs[2].astype(f32) + bufs[5].astype(f32))
    for cp in (a, b, c, d, e, f):
        cp.wait_send()


def plane_scatter(part, res, big, mid, small, h, ss, rs):
    base, q = h * 1024, 512

    def keep(s, v):
        mid[:, :, s * q : (s + 1) * q] = v.astype(bf16)

    def final(s, v):
        res[:, base + s * q : base + (s + 1) * q] = v

    cols = [slice(base + s * q, base + (s + 1) * q) for s in (0, 1)]
    sub = [slice(s * q, (s + 1) * q) for s in (0, 1)]
    if h == 0:
        yield from ring_scatter("x", lambda i, s: part.at[i, :, :, cols[s]], big, keep, ss.at[0], rs.at[0])
        yield from ring_scatter("y", lambda i, s: mid.at[i, :, sub[s]], small, final, ss.at[1], rs.at[1])
    else:
        yield from ring_scatter("y", lambda i, s: part.at[:, i, :, cols[s]], big, keep, ss.at[0], rs.at[0])
        yield from ring_scatter("x", lambda i, s: mid.at[i, :, sub[s]], small, final, ss.at[1], rs.at[1])


def plane_sum(part, acc, big, mid, small, ss, rs):
    yield from together(
        plane_scatter(part, acc, big.at[h], mid.at[h], small.at[h], h, ss.at[h], rs.at[h]) for h in (0, 1)
    )


SCATTER_SCRATCH = [
    pltpu.VMEM((2, 6, 4, 32, 512), bf16),
    pltpu.VMEM((2, 4, 32, 1024), bf16),
    pltpu.VMEM((2, 6, 32, 512), bf16),
    pltpu.SemaphoreType.DMA((2, 2, 6)),
    pltpu.SemaphoreType.DMA((2, 2, 6)),
]
VM = pl.BlockSpec(memory_space=pltpu.VMEM)
SM = pl.BlockSpec(memory_space=pltpu.SMEM)
HB = pl.BlockSpec(memory_space=pl.ANY)


def shape(dims, kind=f32):
    return jax.ShapeDtypeStruct(dims, kind)


def remote_params(cid):
    return pltpu.CompilerParams(collective_id=cid, has_side_effects=True, vmem_limit_bytes=VLIM)


def columns(r):
    return lambda yy: r.at[:, :, lanes(lax.axis_index("x"), yy)]


def slots(r):
    return lambda yy: r.at[yy]


def pick_flow(src, every, index, out, skip, es, er, gs, gr):
    x, y = lax.axis_index("x"), lax.axis_index("y")
    yield from exchange_flow(columns(src), every, es, er)
    here = lanes(x, y)

    def block(j):
        a = index[j]
        return every[a >> 4, (a >> 2) & 3, (a >> 1) & 1, a & 1]

    if skip:
        out[0:skip, here] = block(0)[STRETCH - skip : STRETCH]
    for j in range(8):
        out[skip + 64 * j : skip + 64 * (j + 1), here] = block(j + 1)
    yield from gather_columns(out, skip, gs, gr)


PICK_SCRATCH = [
    pltpu.VMEM((4, 4, 2, 2, 64, 128), bf16),
    pltpu.SemaphoreType.DMA((15,)),
    pltpu.SemaphoreType.DMA((15,)),
] + GATHER_SEMS


def spread_gain(line, row, out):
    for i in range(32):
        out[:, 64 * i : 64 * (i + 1)] = line[i // 8, i // 2 % 4, i % 2, row : row + 1, 0:64]


def fetch(order, tokens, pack, tiny, cid):
    def kernel(order, tok, pack, tiny, wa, line, index, gain1, gain2, xr, h1, xo, every, es, er, gs, gr, ss, rs):
        x, y, z, c = (lax.axis_index(a) for a in "xyzc")
        seg = z * 2 + c

        def find(a, found):
            return tuple(jnp.where(order[a] == jnp.maximum(seg * 8 - 1 + j, 0), a, f) for j, f in enumerate(found))

        for j, f in enumerate(lax.fori_loop(0, 64, find, tuple(jnp.int32(0) for _ in range(9)))):
            index[j] = f
        greet(peers(y=(1, 2, 3), z=(1, 3), c=(1,), x=(1, 3)))

        def rows():
            yield from pick_flow(tok, every, index, xo, HALO, es, er, gs, gr)

            def norm(t, _):
                at_rows = pl.ds(pl.multiple_of(t * 16, 16), 16)
                v = xo[at_rows, :].astype(f32)
                r = lax.rsqrt(jnp.mean(v * v, axis=-1, keepdims=True) + EPS)
                h1[at_rows, :] = (v * r * gain1[...]).astype(bf16)
                return 0

            lax.fori_loop(0, ROWS // 16, norm, 0)
            xr[...] = xo[pl.ds(pl.multiple_of(HALO + 32 * (x * 4 + y), 16), 32), :]

        def small():
            yield from exchange_flow(slots(tiny), line, ss.at[0], rs.at[0])
            spread_gain(line, 1, gain1)
            spread_gain(line, 2, gain2)

        run([rows(), small(), exchange_flow(slots(pack), wa, ss.at[1], rs.at[1])], "012" + "01" * 6 + "2" + "02" * 3)

    return pl.pallas_call(
        kernel,
        out_shape=[
            shape((4, 4, 2) + pack.shape[1:], bf16),
            shape((4, 4, 2) + tiny.shape[1:]),
            shape((16,), i32),
            shape((1, D)),
            shape((1, D)),
            shape((32, D), bf16),
            shape((ROWS, D), bf16),
        ],
        in_specs=[SM] + [VM] * 3,
        out_specs=[VM] * 2 + [SM] + [VM] * 4,
        scratch_shapes=[pltpu.VMEM((ROWS, D), bf16)]
        + PICK_SCRATCH
        + [pltpu.SemaphoreType.DMA((2, 15)), pltpu.SemaphoreType.DMA((2, 15))],
        compiler_params=remote_params(cid),
    )(order, tokens, pack, tiny)


def sum_norm_gather(part, xrows, gain, wpart, cid):
    def kernel(part, xr, gain, wp, m_out, h_out, w_out, acc, big, mid, small, ss, rs, gs, gr, ws, wr, ls):
        x, y, z, c = (lax.axis_index(a) for a in "xyzc")
        own = pltpu.make_async_copy(wp, w_out.at[:, z, c], ls)
        own.start()
        greet(peers(x=(1, 3), y=(1, 3), z=(1, 3), c=(1,)))

        def rows():
            yield from plane_sum(part, acc, big, mid, small, ss, rs)
            m = xr[...].astype(f32) + acc[...]
            m_out[...] = m
            r = lax.rsqrt(jnp.mean(m * m, axis=-1, keepdims=True) + EPS)
            h_out[x, y] = (m * r * gain[...]).astype(bf16)
            yield from gather_rows(h_out, gs, gr)

        def weights():
            own.wait()
            yield from spread_flow(w_out, ws, wr)

        run([rows(), weights()], "01000100010")

    return pl.pallas_call(
        kernel,
        out_shape=[
            shape((32, D)),
            shape((4, 4, 32, D), bf16),
            shape((4, 4, 2) + wpart.shape[1:], bf16),
        ],
        in_specs=[VM] * 4,
        out_specs=[VM] * 3,
        scratch_shapes=[pltpu.VMEM((32, D), f32)]
        + SCATTER_SCRATCH
        + GATHER_SEMS
        + [pltpu.SemaphoreType.DMA((11,)), pltpu.SemaphoreType.DMA((11,)), pltpu.SemaphoreType.DMA],
        compiler_params=remote_params(cid),
    )(part, xrows, gain, wpart)


def norm_back(v, gain, dh):
    r = lax.rsqrt(jnp.mean(v * v, axis=-1, keepdims=True) + EPS)
    t = gain * dh
    dv = r * t - v * (r * r * r) * jnp.mean(v * t, axis=-1, keepdims=True)
    return dv, jnp.sum(v * r * dh, axis=0, keepdims=True)


def back_middle(part, m, dyrows, gain, grads, cid):
    n = len(grads)

    def kernel(part, m, dy, gain, *refs):
        gin, (dm_out, dg_out, da_out), gout = refs[:n], refs[n : n + 3], refs[n + 3 : 2 * n + 3]
        acc, big, mid, small, ss, rs, gs, gr = refs[2 * n + 3 : 2 * n + 11]
        rest = refs[2 * n + 11 :]
        x, y = lax.axis_index("x"), lax.axis_index("y")
        greet(peers(x=(1, 3), y=(1, 3), z=(1, 3), c=(1,)))

        def rows():
            yield from plane_sum(part, acc, big, mid, small, ss, rs)
            dv, dgain = norm_back(m[...], gain[...], acc[...])
            dm = dy[...].astype(f32) + dv
            dm_out[...] = dm
            dg_out[...] = dgain
            da_out[x, y] = dm.astype(bf16)
            yield from gather_rows(da_out, gs, gr)

        def sums():
            yield from together(sum_flow(gin[i], gout[i], *rest[4 * i : 4 * i + 4]) for i in range(n))

        run([rows(), sums()], "0100100100")

    return pl.pallas_call(
        kernel,
        out_shape=[shape((32, D)), shape((1, D)), shape((4, 4, 32, D), bf16)]
        + [shape((4,) + g.shape[3:], bf16) for g in grads],
        in_specs=[VM] * (4 + n),
        out_specs=[VM] * (3 + n),
        scratch_shapes=[pltpu.VMEM((32, D), f32)]
        + SCATTER_SCRATCH
        + GATHER_SEMS
        + [r for g in grads for r in sum_scratch(g.shape[3:], bf16)],
        compiler_params=remote_params(cid),
    )(part, m, dyrows, gain, *grads)


def home_flow(src, dst, order, alls, cols, picks, s1, r1, s2, r2, s3, r3):
    x, y, z, c = (lax.axis_index(a) for a in "xyzc")
    sends = []
    cols[x, y] = src[:, pl.ds(pl.multiple_of((x * 4 + y) * 128, 128), 128)]
    t = 0
    for i in range(4):
        for j in range(4):
            if (i, j) == (0, 0):
                continue
            px, py = at("x", i), at("y", j)
            lane = pl.multiple_of((px * 4 + py) * 128, 128)
            sends.append(send(src.at[:, pl.ds(lane, 128)], cols.at[x, y], s1.at[t], r1.at[t], {"x": px, "y": py}))
            t += 1
    yield
    for cp in sends:
        cp.wait_recv()
    alls[z, c] = cols[...].reshape(8, 64, 128)
    yield from zc_gather(
        lambda zz, cc: alls.at[zz, cc], lambda zz, cc: (alls.at[zz, cc, 0:4], alls.at[zz, cc, 4:8]), s2, r2
    )
    for j in range(4):
        for i in range(2):
            b = order[j * 16 + (z * 2 + c) * 2 + i]
            picks[j, 64 * i : 64 * (i + 1)] = alls[b >> 4, (b >> 3) & 1, b & 7]
    mine = pl.ds(pl.multiple_of(y * 128, 128), 128)
    last = [
        send(picks.at[at("y", j)], dst.at[:, mine], s3.at[j], r3.at[j], {"y": at("y", j)}) for j in (2, 1, 3)
    ]
    dst[:, mine] = picks[y]
    yield
    for cp in last:
        cp.wait_recv()
    for cp in sends + last:
        cp.wait_send()


HOME_SCRATCH = [
    pltpu.VMEM((4, 2, 8, 64, 128), bf16),
    pltpu.VMEM((4, 4, 32, 128), bf16),
    pltpu.VMEM((4, 128, 128), bf16),
    pltpu.SemaphoreType.DMA((15,)),
    pltpu.SemaphoreType.DMA((15,)),
    pltpu.SemaphoreType.DMA((11,)),
    pltpu.SemaphoreType.DMA((11,)),
    pltpu.SemaphoreType.DMA((4,)),
    pltpu.SemaphoreType.DMA((4,)),
]


def sum_flow(g, stage, core, bufs, ss, rs):
    c = lax.axis_index("c")
    d = send(g.at[:, :, 1 - c], core, ss.at[0], rs.at[0], {"c": 1 - c})
    yield
    d.wait_recv()

    def add(i, _):
        core[i] = (core[i].astype(f32) + g[i, :, c].astype(f32)).astype(core.dtype)
        return 0

    lax.fori_loop(0, 4, add, 0)

    def emit(s, v):
        stage[2 * s : 2 * s + 2] = v.astype(stage.dtype)

    yield from ring_scatter(
        "z", lambda i, s: core.at[2 * s : 2 * s + 2, i], bufs, emit, ss.at[pl.ds(1, 6)], rs.at[pl.ds(1, 6)]
    )
    d.wait_send()


def sum_scratch(dims, kind):
    return [
        pltpu.VMEM((4, 4) + dims, kind),
        pltpu.VMEM((6, 2) + dims, kind),
        pltpu.SemaphoreType.DMA((7,)),
        pltpu.SemaphoreType.DMA((7,)),
    ]


TRADE_SEMS = [pltpu.SemaphoreType.DMA((4,)), pltpu.SemaphoreType.DMA((4,))]


def scatter_flow(g, out, stage, ts, tr, *sums):
    yield from sum_flow(g, stage, *sums)
    yield from trade_flow(slots(stage), lambda y: out.at[y], ts, tr)


def scatter_scratch(dims, kind):
    return [pltpu.VMEM((4,) + dims, kind)] + TRADE_SEMS + sum_scratch(dims, kind)


def finish(order, part, xrows, dm, gain, grad, tiny, cid):
    nh, ns = len(HOME_SCRATCH), 7

    def kernel(order, part, xr, dm, gain, grad, tiny, dt_out, g_out, t_out, tot, acc, *rest):
        big, mid, small, ss, rs = rest[:5]
        home, rest = rest[5 : 5 + nh], rest[5 + nh :]
        ga, ti, rest = rest[:ns], rest[ns : 2 * ns], rest[2 * ns :]
        line, dx, xr4, xs, xq = rest
        x = lax.axis_index("x")
        greet(plane_peers() + peers(z=(1, 3), c=(1,)))

        def small_grads():
            yield from scatter_flow(line, t_out, *ti)
            xr4[x] = (t_out[0] + t_out[1]) + (t_out[2] + t_out[3])
            sends = [send(xr4.at[x], xr4.at[x], xs.at[k], xq.at[k], {"x": at("x", k)}) for k in (2, 1, 3)]
            yield
            for cp in sends:
                cp.wait_recv()
            tot[...] = (xr4[0] + xr4[1]) + (xr4[2] + xr4[3])
            for cp in sends:
                cp.wait_send()

        def input_grads():
            yield from plane_sum(part, acc, big, mid, small, ss, rs)
            dv, dgain = norm_back(xr[...].astype(f32), gain[...], acc[...])
            dx[...] = (dm[...] + dv).astype(bf16)
            line[...] = tiny[...]
            for i in range(32):
                line[i // 8, i // 2 % 4, i % 2, 1:2, 0:64] = dgain[:, 64 * i : 64 * (i + 1)]
            yield from together([home_flow(dx, dt_out, order, *home), small_grads()])

        run([input_grads(), scatter_flow(grad, g_out, *ga)], "0101001")

    td, gd = tiny.shape[3:], grad.shape[3:]
    return pl.pallas_call(
        kernel,
        out_shape=[shape((128, 512), bf16), shape((4,) + gd, bf16), shape((4,) + td), shape(td)],
        in_specs=[SM] + [VM] * 6,
        out_specs=[VM] * 4,
        scratch_shapes=[pltpu.VMEM((32, D), f32)]
        + SCATTER_SCRATCH
        + HOME_SCRATCH
        + scatter_scratch(gd, bf16)
        + scatter_scratch(td, f32)
        + [
            pltpu.VMEM(tiny.shape, f32),
            pltpu.VMEM((32, D), bf16),
            pltpu.VMEM((4,) + td, f32),
            pltpu.SemaphoreType.DMA((4,)),
            pltpu.SemaphoreType.DMA((4,)),
        ],
        compiler_params=remote_params(cid),
    )(order, part, xrows, dm, gain, grad, tiny)


def dot(a, b, dims, prec=None):
    return lax.dot_general(a, b, (dims, ((), ())), preferred_element_type=f32, precision=prec)


def lo(a):
    return a.astype(bf16)


def mm(a, b):
    return dot(lo(a), lo(b), ((1,), (0,)))


def mmt(a, b):
    return dot(lo(a), lo(b), ((1,), (1,)))


def tmm(a, b):
    return dot(lo(a), lo(b), ((0,), (0,)))


def halves_of(a):
    h = a.astype(bf16)
    return h, (a - h.astype(f32)).astype(bf16)


def fine(a, b, dims=((1,), (0,))):
    ah, al = halves_of(a)
    bh, bl = halves_of(b)
    return dot(ah, bh, dims) + (dot(ah, bl, dims) + dot(al, bh, dims))


def tri_inverse(a, r, c):
    eye = jnp.where(r == c, 1.0, 0.0)
    n1 = jnp.where((r >> 3) == (c >> 3), -a, 0.0)
    n2 = fine(n1, n1)
    n4 = fine(n2, n2)
    t = eye + n1
    t = t + fine(t, n2)
    t = t + fine(t, n4)
    for level in (3, 4, 5, 6):
        off = ((r >> (level + 1)) == (c >> (level + 1))) & ((r >> level) != (c >> level))
        t = t - fine(t, fine(jnp.where(off, a, 0.0), t))
    return t


def iotas():
    return (
        lax.broadcasted_iota(i32, (CH, CH), 0),
        lax.broadcasted_iota(i32, (CH, CH), 1),
    )


def filtered(z, cw, mc, cols):
    total = z[HALO : HALO + SEG, cols] * cw[3:4, cols]
    for j in range(3):
        total = total + mc[:, j : j + 1] * cw[j : j + 1, cols] * z[HALO - 3 + j : HALO - 3 + j + SEG, cols]
    return total


def silu(v):
    return v * jax.nn.sigmoid(v)


QC, KC, VC = slice(0, 128), slice(128, 256), slice(256, 512)


def decay_of(cc, cr, mask):
    return jnp.exp(jnp.where(mask, cc - cr, 0.0)) * jnp.where(mask, 1.0, 0.0)


def prepare(z, ab, cw, sc, mc, mr, qkv, tm, wu, gb, cr, ti):
    r, c = iotas()
    for cols, scale in ((QC, DK**-0.5), (KC, 1.0)):
        s = silu(filtered(z, cw, mc, cols))
        qkv[:, cols] = (s * lax.rsqrt(jnp.sum(s * s, axis=-1, keepdims=True) + EPS) * scale).astype(bf16)
    qkv[:, VC] = silu(filtered(z, cw, mc, VC)).astype(bf16)
    low = jnp.where(r >= c, 1.0, 0.0)
    eye = jnp.where(r == c, 1.0, 0.0)
    lane = lax.broadcasted_iota(i32, (CH, 128), 1)
    transit = eye
    insert = jnp.zeros((DK, DV), f32)
    yield
    for n in range(NCH):
        rows = slice(n * CH, (n + 1) * CH)
        raw = ab[HALO + n * CH : HALO + (n + 1) * CH, :]
        beta = jax.nn.sigmoid(raw[:, 1:2])
        u = raw + sc[0:1, 1:2]
        g = -jnp.exp(sc[0:1, 0:1]) * (jnp.maximum(u, 0.0) + jnp.log1p(jnp.exp(-jnp.abs(u))))
        g = jnp.where(lane == 0, g, 0.0)
        cum = dot(low, g, ((1,), (0,)), HI)[:, 0:1]
        cumr = dot(g, low, ((0,), (1,)), HI)[0:8, :]
        gb[rows, :] = jnp.where(lane == 0, beta, cum)
        cr[:, rows] = cumr
        cumrow = cumr[0:1, :]
        last = cumr[0:1, CH - 1 : CH]
        m = mc[rows, :]
        carried, closing, begin, carry_last = m[:, 3:4], m[:, 4:5], m[:, 5:6], m[0:1, 6:7]
        same = begin == mr[0:1, rows]
        k = qkv[rows, KC]
        kf = k.astype(f32)
        v = qkv[rows, VC].astype(f32)
        a = beta * dot(k, k, ((1,), (1,))) * decay_of(cum, cumrow, same & (r > c))
        t = tri_inverse(a, r, c)
        tm[rows, :] = t
        lead = (beta * jnp.exp(cum) * carried) * kf
        w = fine(t, lead)
        uu = fine(t, beta * v)
        wu[rows, 0:DK] = w
        wu[rows, DK:] = uu
        tail = kf * (jnp.exp(last - cum) * closing)
        keep = jnp.exp(last) * carry_last
        hand = keep * eye - fine(tail, w, ((0,), (0,)))
        insert = fine(hand, insert) + fine(tail, uu, ((0,), (0,)))
        transit = fine(hand, transit)
        yield
    ti[:, 0:DK] = transit.astype(bf16)
    ti[:, DK:] = insert.astype(bf16)


def emit_outputs(seg, maps, qkv, wu, gb, cr, mc, mr, gp, hg, nout, oout, fout, sout):
    r, c = iotas()

    def fold(d, s):
        tr, ins = maps[d, :, 0:DK], maps[d, :, DK:].astype(f32)
        sh, sl = halves_of(s)
        new = dot(tr, sh, ((1,), (0,))) + dot(tr, sl, ((1,), (0,))) + ins
        return jnp.where(d < seg, new, s)

    s = lax.fori_loop(0, 7, fold, jnp.zeros((DK, DV), f32))
    for n in range(NCH):
        rows = slice(n * CH, (n + 1) * CH)
        m = mc[rows, :]
        carried, closing, begin, carry_last = m[:, 3:4], m[:, 4:5], m[:, 5:6], m[0:1, 6:7]
        cum = gb[rows, 1:2]
        cumrow = cr[0:1, rows]
        last = cr[0:1, n * CH + CH - 1 : n * CH + CH]
        same = begin == mr[0:1, rows]
        q, k = qkv[rows, QC], qkv[rows, KC]
        p = dot(q, k, ((1,), (1,))) * decay_of(cum, cumrow, same & (r >= c))
        fresh = wu[rows, DK:] - fine(wu[rows, 0:DK], s)
        qd = q.astype(f32) * (jnp.exp(cum) * carried)
        o = mm(qd, s) + mm(p, fresh)
        sout[n] = s
        fout[rows, :] = fresh
        oout[rows, :] = o
        x = gp[HALO + n * CH : HALO + (n + 1) * CH, :]
        rn = lax.rsqrt(jnp.mean(o * o, axis=-1, keepdims=True) + EPS)
        nout[rows, :] = (o * rn * hg[0:1, :] * silu(x)).astype(bf16)
        tail = k.astype(f32) * (jnp.exp(last - cum) * closing)
        s = (jnp.exp(last) * carry_last) * s + fine(tail, fresh, ((0,), (0,)))
        yield


def back_emit(dn, o, gp, hg, qkv, wu, gb, cr, mc, mr, do_out, dgp_out, dhg_out, e_out):
    r, c = iotas()
    dhg = jnp.zeros((1, DV), f32)
    e = jnp.zeros((DK, DV), f32)
    for n in reversed(range(NCH)):
        rows = slice(n * CH, (n + 1) * CH)
        ov, x, dnv = o[rows, :], gp[HALO + n * CH : HALO + (n + 1) * CH, :], dn[rows, :]
        rn = lax.rsqrt(jnp.mean(ov * ov, axis=-1, keepdims=True) + EPS)
        sg = jax.nn.sigmoid(x)
        act = x * sg
        h = hg[0:1, :]
        base = ov * rn
        dhg = dhg + jnp.sum(base * act * dnv, axis=0, keepdims=True)
        dgp_out[rows, :] = (dnv * base * h * (sg * (1.0 + x * (1.0 - sg)))).astype(bf16)
        t = dnv * h * act
        do = rn * t - base * (rn * rn) * jnp.mean(ov * t, axis=-1, keepdims=True)
        do_out[rows, :] = do
        m = mc[rows, :]
        carried, closing, begin, carry_last = m[:, 3:4], m[:, 4:5], m[:, 5:6], m[0:1, 6:7]
        cum = gb[rows, 1:2]
        cumrow = cr[0:1, rows]
        last = cr[0:1, n * CH + CH - 1 : n * CH + CH]
        same = begin == mr[0:1, rows]
        q, k = qkv[rows, QC], qkv[rows, KC]
        p = dot(q, k, ((1,), (1,))) * decay_of(cum, cumrow, same & (r >= c))
        qd = q.astype(f32) * (jnp.exp(cum) * carried)
        tail = k.astype(f32) * (jnp.exp(last - cum) * closing)
        df = tmm(p, do) + mm(tail, e)
        e = tmm(qd, do) + (jnp.exp(last) * carry_last) * e - tmm(wu[rows, 0:DK], df)
        yield
    dhg_out[...] = dhg
    e_out[...] = e.astype(bf16)


def back_delta(seg, maps, tails, do, fr, st, qkv, tm, wu, gb, cr, z, ab, cw, sc, mc, mr, dz, dab, dcw, dsc, dqkv):
    r, c = iotas()
    low = jnp.where(r >= c, 1.0, 0.0)
    ones = jnp.ones((CH, CH), f32)
    lane = lax.broadcasted_iota(i32, (CH, 128), 1)
    row = lax.broadcasted_iota(i32, (CH, 1), 0)

    def fold(i, e):
        d = 7 - i
        tr, own = maps[d, :, 0:DK], tails[d].astype(f32)
        eh, el = halves_of(e)
        new = dot(tr, eh, ((0,), (0,))) + dot(tr, el, ((0,), (0,))) + own
        return jnp.where(d > seg, new, e)

    e = lax.fori_loop(0, 7, fold, jnp.zeros((DK, DV), f32))
    acc_a = jnp.zeros((1, 128), f32)
    acc_d = jnp.zeros((1, 128), f32)
    for n in reversed(range(NCH)):
        rows = slice(n * CH, (n + 1) * CH)
        m = mc[rows, :]
        carried, closing, begin, carry_last = m[:, 3:4], m[:, 4:5], m[:, 5:6], m[0:1, 6:7]
        beta, cum = gb[rows, 0:1], gb[rows, 1:2]
        cumrow = cr[0:1, rows]
        last = cr[0:1, n * CH + CH - 1 : n * CH + CH]
        same = begin == mr[0:1, rows]
        q, k = qkv[rows, QC], qkv[rows, KC]
        qf, kf, vf = q.astype(f32), k.astype(f32), qkv[rows, VC].astype(f32)
        dec_i = decay_of(cum, cumrow, same & (r >= c))
        dec_s = jnp.where(r > c, dec_i, 0.0)
        p = dot(q, k, ((1,), (1,))) * dec_i
        kkd = dot(k, k, ((1,), (1,))) * dec_s
        ex = jnp.exp(cum) * carried
        tf = jnp.exp(last - cum) * closing
        keep = jnp.exp(last) * carry_last
        tail = kf * tf
        qd = qf * ex
        dov, fv, sv, tv = do[rows, :], fr[rows, :], st[n], tm[rows, :]
        w, u = wu[rows, 0:DK], wu[rows, DK:]
        df = tmm(p, dov) + mm(tail, e)
        dw = -mmt(df, sv)
        dtail = mmt(fv, e)
        dkeep = jnp.sum(jnp.sum(sv * e, axis=1, keepdims=True), axis=0, keepdims=True)
        dqd = mmt(dov, sv)
        dp = mmt(dov, fv)
        dlead = tmm(tv, dw)
        dbv = tmm(tv, df)
        da = -(mmt(dlead, w) + mmt(dbv, u))
        dakd = da * kkd
        dkk = da * beta * dec_s
        dqk = dp * dec_i
        mix = dakd * beta + dp * p
        dqkv[rows, QC] = mm(dqk, k) + dqd * ex
        dqkv[rows, KC] = (
            tmm(dqk, q) + mm(dkk, k) + tmm(dkk, k) + dlead * (beta * ex) + dtail * tf
        )
        dqkv[rows, VC] = beta * dbv
        lk = jnp.sum(dlead * kf, axis=1, keepdims=True) * ex
        dbeta = jnp.sum(dakd, axis=1, keepdims=True) + lk + jnp.sum(dbv * vf, axis=1, keepdims=True)
        tt = jnp.sum(dtail * tail, axis=1, keepdims=True)
        dcum = jnp.sum(mix, axis=1, keepdims=True) + jnp.sum(dqd * qd, axis=1, keepdims=True) + lk * beta - tt
        dcum = dcum + jnp.where(row == CH - 1, jnp.sum(tt, axis=0, keepdims=True) + dkeep * keep, 0.0)
        full = dcum - dot(mix, ones, ((0,), (0,)), HI)
        dg = dot(low, full, ((0,), (0,)), HI)
        raw = ab[HALO + n * CH : HALO + (n + 1) * CH, :]
        uu = raw + sc[0:1, 1:2]
        rate = -jnp.exp(sc[0:1, 0:1])
        sp = jnp.maximum(uu, 0.0) + jnp.log1p(jnp.exp(-jnp.abs(uu)))
        dal = dg * rate * jax.nn.sigmoid(uu)
        acc_a = acc_a + jnp.sum(dg * rate * sp, axis=0, keepdims=True)
        acc_d = acc_d + jnp.sum(dal, axis=0, keepdims=True)
        dab[rows, :] = jnp.where(
            lane == 0, dal, jnp.where(lane == 1, dbeta * beta * (1.0 - beta), 0.0)
        ).astype(bf16)
        e = tmm(qd, dov) + keep * e - tmm(w, df)
        yield
    dsc[0:1, :] = acc_a
    dsc[1:2, :] = acc_d
    dz[0:HALO, :] = jnp.zeros((HALO, 512), f32)
    for cols, scale in ((QC, DK**-0.5), (KC, 1.0), (VC, None)):
        y = filtered(z, cw, mc, cols)
        sg = jax.nn.sigmoid(y)
        ds = dqkv[:, cols]
        if scale is not None:
            s = y * sg
            rn = lax.rsqrt(jnp.sum(s * s, axis=-1, keepdims=True) + EPS)
            ds = scale * (rn * ds - s * (rn * rn * rn) * jnp.sum(s * ds, axis=-1, keepdims=True))
        dy = ds * (sg * (1.0 + y * (1.0 - sg)))
        dz[HALO : HALO + SEG, cols] = dy * cw[3:4, cols]
        dcw[3:4, cols] = jnp.sum(dy * z[HALO : HALO + SEG, cols], axis=0, keepdims=True)
        for j in range(3):
            part = mc[:, j : j + 1] * dy
            away = slice(HALO - 3 + j, HALO - 3 + j + SEG)
            dcw[j : j + 1, cols] = jnp.sum(part * z[away, cols], axis=0, keepdims=True)
            dz[away, cols] = dz[away, cols] + part * cw[j : j + 1, cols]
        yield


def map_gather(own, out, ss, rs):
    z, c = lax.axis_index("z"), lax.axis_index("c")
    out[z, c] = own[...]
    h = own.shape[0] // 2
    yield from zc_gather(
        lambda zz, cc: out.at[zz, cc], lambda zz, cc: (out.at[zz, cc, 0:h], out.at[zz, cc, h : 2 * h]), ss, rs
    )


class Maps:
    def __init__(self, ref):
        self.ref = ref

    def __getitem__(self, key):
        key = key if isinstance(key, tuple) else (key,)
        return self.ref[(key[0] // 2, key[0] % 2) + key[1:]]


def masks(lens, mc, mr):
    base = (lax.axis_index("z") * 2 + lax.axis_index("c")) * SEG
    firsts = [jnp.int32(0)]
    for k in range(3):
        firsts.append(firsts[k] + lens[k])

    def begin_of(pos):
        b = jnp.zeros_like(pos)
        for k in range(1, 4):
            b = jnp.where((pos >= firsts[k]) & (pos < firsts[k] + lens[k]), firsts[k], b)
        return b

    lane = lax.broadcasted_iota(i32, (CH, 128), 1)
    for n in range(NCH):
        first = base + n * CH
        pos = first + lax.broadcasted_iota(i32, (CH, 128), 0)
        b = begin_of(pos)
        last = begin_of(jnp.full((CH, 128), first + CH - 1, i32))

        def one(flag):
            return jnp.where(flag, 1.0, 0.0)

        late = jnp.where(lane == 3, one(b < first), jnp.where(lane == 4, one(b == last), one(last < first)))
        flags = jnp.where(lane < 3, one(pos - 3 + lane >= b), late)
        mc[n * CH : (n + 1) * CH, :] = jnp.where(lane == 5, b.astype(f32), flags)
        mr[:, n * CH : (n + 1) * CH] = begin_of(first + lax.broadcasted_iota(i32, (8, CH), 1)).astype(f32)


def attend(proj, cw, hg, lens, a_log, dt_bias, index, cotangent, pack, cid):
    npk = len(PICK_SCRATCH)

    def kernel(proj, cw, hg, lens, al, dt, index, cot, pack, wp, dyo, dyr, qkv, tm, wu, gb, cr, maps, nout, oout, fout, sout, mc, mr, sc, *refs):
        every, es, er, gs, gr = refs[:npk]
        ti, ms, mq, ts, tr = refs[npk:]
        x, y, z, c = (lax.axis_index(a) for a in "xyzc")
        zq, gp, ab = proj.at[:, 0:512], proj.at[:, 512:768], proj.at[:, 768:896]
        greet(peers(y=(1, 2, 3), z=(1, 3), c=(1,), x=(1, 3)))

        def mixer():
            masks(lens, mc, mr)
            sc[0:8, :] = jnp.where(lax.broadcasted_iota(i32, (8, 128), 1) == 0, al[y], dt[y])
            yield from prepare(zq, ab, cw, sc, mc, mr, qkv, tm, wu, gb, cr, ti)
            yield from map_gather(ti, maps, ms, mq)
            yield from emit_outputs(z * 2 + c, Maps(maps), qkv, wu, gb, cr, mc, mr, gp, hg, nout, oout, fout, sout)

        def cotangents():
            yield from pick_flow(cot, every, index, dyo, 0, es, er, gs, gr)
            dyr[...] = dyo[pl.ds(pl.multiple_of(32 * (x * 4 + y), 32), 32), :]

        run(
            [mixer(), cotangents(), trade_flow(slots(pack), lambda i: wp.at[i], ts, tr)],
            "12" + "01" * 5 + "0011" + "0101" * 4,
        )

    return pl.pallas_call(
        kernel,
        out_shape=[
            shape(pack.shape, bf16),
            shape((SEG, D), bf16),
            shape((32, D), bf16),
            shape((SEG, 512), bf16),
            shape((SEG, CH)),
            shape((SEG, DK + DV)),
            shape((SEG, 128)),
            shape((8, SEG)),
            shape((4, 2, DK, DK + DV), bf16),
            shape((SEG, DV), bf16),
            shape((SEG, DV)),
            shape((SEG, DV)),
            shape((NCH, DK, DV)),
            shape((SEG, 128)),
            shape((8, SEG)),
            shape((8, 128)),
        ],
        in_specs=[VM] * 3 + [SM] * 4 + [VM] * 2,
        out_specs=[VM] * 16,
        scratch_shapes=PICK_SCRATCH
        + [
            pltpu.VMEM((DK, DK + DV), bf16),
            pltpu.SemaphoreType.DMA((11,)),
            pltpu.SemaphoreType.DMA((11,)),
        ]
        + TRADE_SEMS,
        compiler_params=remote_params(cid),
    )(proj, cw, hg, lens, a_log, dt_bias, index, cotangent, pack)


def back_attend(dn, o, proj, hg, qkv, tm, wu, gb, cr, mc, mr, maps, fr, st, cw, sc, m, order, ypart, stages, grad, cid):
    nh, n = len(HOME_SCRATCH), len(stages)

    def kernel(dn, o, proj, hg, qkv, tm, wu, gb, cr, mc, mr, maps, fr, st, cw, sc, m, order, ypart, *refs):
        staged, grad, refs = refs[:n], refs[n], refs[n + 1 :]
        y_out, dproj, dhg, dcw, dsc, g_out = refs[:6]
        s_out, refs = refs[6 : 6 + n], refs[6 + n :]
        do, dgp, e, tails, dz, dab, dqkv, edge, ms, mq, ds, dq, acc, yrow = refs[:14]
        big, mid, small, ss, rs = refs[14:19]
        home, refs = refs[19 : 19 + nh], refs[19 + nh :]
        ga, trades = refs[:7], refs[7:]
        zq, gp, ab = proj.at[:, 0:512], proj.at[:, 512:768], proj.at[:, 768:896]
        seg = lax.axis_index("z") * 2 + lax.axis_index("c")
        greet(plane_peers() + segment_peers())

        def mixer():
            yield from back_emit(dn, o, gp, hg, qkv, wu, gb, cr, mc, mr, do, dgp, dhg, e)
            yield from map_gather(e, tails, ms, mq)
            yield from back_delta(
                seg, Maps(maps), Maps(tails), do, fr, st, qkv, tm, wu, gb, cr, zq, ab, cw, sc, mc, mr, dz, dab, dcw, dsc, dqkv
            )
            before = lax.rem(seg + 7, 8)
            cp = send(dz.at[0:HALO], edge, ds, dq, {"z": before // 2, "c": lax.rem(before, 2)})
            dproj[0 : SEG - HALO, 0:512] = dz[HALO:SEG].astype(bf16)
            dproj[:, 512:768] = dgp[...]
            dproj[:, 768:896] = dab[...]
            yield
            cp.wait_recv()
            dproj[SEG - HALO : SEG, 0:512] = (dz[SEG:ROWS] + jnp.where(seg < 7, edge[...], 0.0)).astype(bf16)
            cp.wait_send()

        def result():
            yield from plane_sum(ypart, acc, big, mid, small, ss, rs)
            yrow[...] = (m[...] + acc[...]).astype(bf16)
            yield from home_flow(yrow, y_out, order, *home)

        def trade(i):
            return trade_flow(slots(staged[i]), lambda y: s_out[i].at[y], trades[2 * i], trades[2 * i + 1])

        run(
            [mixer(), result(), scatter_flow(grad, g_out, *ga)] + [trade(i) for i in range(n)],
            "12" + "0" * 4 + "12" + "0" * 2 + "12" + "0" * 2 + "12" + "34"[:n] + "0" * 2 + "12" + "0" + "12" + "0" + "34"[:n] + "012012012",
        )

    gd = grad.shape[3:]
    return pl.pallas_call(
        kernel,
        out_shape=[
            shape((128, 512), bf16),
            shape((SEG, 896), bf16),
            shape((1, DV)),
            shape((4, 512)),
            shape((2, 128)),
            shape((4,) + gd, bf16),
        ]
        + [shape(t.shape, bf16) for t in stages],
        in_specs=[VM] * 17 + [SM] + [VM] * (2 + n),
        out_specs=[VM] * (6 + n),
        scratch_shapes=[
            pltpu.VMEM((SEG, DV), f32),
            pltpu.VMEM((SEG, DV), bf16),
            pltpu.VMEM((DK, DV), bf16),
            pltpu.VMEM((4, 2, DK, DV), bf16),
            pltpu.VMEM((ROWS, 512), f32),
            pltpu.VMEM((SEG, 128), bf16),
            pltpu.VMEM((SEG, 512), f32),
            pltpu.VMEM((HALO, 512), f32),
            pltpu.SemaphoreType.DMA((11,)),
            pltpu.SemaphoreType.DMA((11,)),
            pltpu.SemaphoreType.DMA,
            pltpu.SemaphoreType.DMA,
            pltpu.VMEM((32, D), f32),
            pltpu.VMEM((32, D), bf16),
        ]
        + SCATTER_SCRATCH
        + HOME_SCRATCH
        + scatter_scratch(gd, bf16)
        + TRADE_SEMS * n,
        compiler_params=remote_params(cid),
    )(dn, o, proj, hg, qkv, tm, wu, gb, cr, mc, mr, maps, fr, st, cw, sc, m, order, ypart, *stages, grad)


def wide(a):
    a = jnp.pad(a.astype(bf16), ((0, 0), (0, 4 * FFP - a.shape[1])))
    return a.reshape(a.shape[0], 4, FFP).swapaxes(0, 1)


def body(
    tokens,
    cotangent,
    seq_lengths,
    stretch_order,
    attn_gain,
    w_query,
    w_key,
    w_value,
    w_alpha,
    w_beta,
    conv_query,
    conv_key,
    conv_value,
    a_log,
    dt_bias,
    head_gain,
    w_outgate,
    w_output,
    mlp_gain,
    w_gate,
    w_up,
    w_down,
):
    ff = w_gate.shape[1]

    def by_head(a):
        return a.astype(bf16).swapaxes(0, 1)

    pair = jnp.stack([w_alpha, w_beta], axis=-1).astype(bf16)
    pack_a = jnp.concatenate(
        [
            by_head(w_query),
            by_head(w_key),
            by_head(w_value),
            by_head(w_outgate),
            jnp.pad(pair.swapaxes(0, 1), ((0, 0), (0, 0), (0, 126))),
            w_output.astype(bf16).swapaxes(1, 2),
        ],
        axis=2,
    )
    pack_b = jnp.concatenate([wide(w_gate), wide(w_up), wide(w_down.T)], axis=2)

    def taps(a):
        return a.swapaxes(0, 1).reshape(4, -1)

    def each(a):
        return jnp.broadcast_to(a[None], (4,) + a.shape)

    line = jnp.concatenate([taps(conv_query), taps(conv_key), taps(conv_value), each(head_gain)], axis=1)
    line = jnp.pad(line, ((0, 0), (0, 128 - line.shape[1])))
    gains = jnp.pad(jnp.stack([attn_gain, mlp_gain]), ((0, 5), (0, 64)))
    tiny = jnp.concatenate([line[:, None], each(gains)], axis=1).astype(bf16).astype(f32)
    wa, lines, index, gain1, gain2, xrows, h1 = fetch(stretch_order, tokens.reshape(2, STRETCH, D), pack_a, tiny, 1)
    wa = wa.reshape(D, NA)
    lines = lines[:, :, :, 0].reshape(32, 128)

    def filters(a):
        return a.reshape(32, 4, -1).swapaxes(0, 1).reshape(4, -1)

    cw = jnp.concatenate([filters(lines[:, 0:16]), filters(lines[:, 16:32]), filters(lines[:, 32:64])], axis=1)
    hg = lines[:, 64:72].reshape(1, DV)

    proj = jnp.dot(h1, wa[:, :896], preferred_element_type=f32)
    wpart, dys, dyrows, qkv, tm, wu, gb, cr, maps, nv, ov, fr, st, mc, mr, sc = attend(
        proj, cw, hg, seq_lengths, a_log, dt_bias, index, cotangent.reshape(2, STRETCH, D), pack_b, 2
    )
    wo = wa[:, 896:]
    part = dot(nv, wo, ((1,), (1,))).astype(bf16).reshape(4, 4, 32, D)
    m, h2, wb = sum_norm_gather(part, xrows, gain2, wpart, 3)
    wb = wb.reshape(D, NB)
    h2 = h2.reshape(SEG, D)
    wg, wu_, wd = wb[:, :FFP], wb[:, FFP : 2 * FFP], wb[:, 2 * FFP :]
    both = jnp.dot(h2, wb[:, : 2 * FFP], preferred_element_type=f32)
    ga, up = both[:, :FFP], both[:, FFP:]
    sg = jax.nn.sigmoid(ga)
    act = ga * sg
    hid = (act * up).astype(bf16)
    ypart = dot(hid, wd, ((1,), (1,))).astype(bf16).reshape(4, 4, 32, D)

    dhid = jnp.dot(dys, wd, preferred_element_type=f32)
    dga = (dhid * up * (sg * (1.0 + ga * (1.0 - sg)))).astype(bf16)
    dup = (dhid * act).astype(bf16)
    dgu = jnp.concatenate([dga, dup], axis=1)
    dh2 = dot(dgu, wb[:, : 2 * FFP], ((1,), (1,))).astype(bf16).reshape(4, 4, 32, D)
    grad_gu = dot(h2, dgu, ((0,), (0,))).astype(bf16).reshape(4, 4, 2, 64, -1)
    grad_d = dot(dys, hid, ((0,), (0,))).astype(bf16).reshape(4, 4, 2, 64, -1)
    dm, dgain2, da, sgu, sd = back_middle(dh2, m, dyrows, gain2, (grad_gu, grad_d), 4)
    da = da.reshape(SEG, D)
    dn = jnp.dot(da, wo, preferred_element_type=f32)
    grad_o = dot(da, nv, ((0,), (0,))).astype(bf16).reshape(4, 4, 2, 64, -1)
    out, dproj, dhg, dcw, dsc, ro, rgu, rd = back_attend(
        dn, ov, proj, hg, qkv, tm, wu, gb, cr, mc, mr, maps, fr, st, cw, sc, m, stretch_order, ypart, (sgu, sd), grad_o, 5
    )
    dh1 = dot(dproj, wa[:, :896], ((1,), (1,))).astype(bf16).reshape(4, 4, 32, D)
    h1o = h1[HALO:]
    grad_a = dot(h1o, dproj, ((0,), (0,))).astype(bf16).reshape(4, 4, 2, 64, -1)
    def unfilter(a):
        return a.reshape(4, 32, -1).swapaxes(0, 1).reshape(32, -1)

    head = jnp.broadcast_to(dsc[:, 0][None], (32, 2))
    back_line = jnp.concatenate(
        [unfilter(dcw[:, QC]), unfilter(dcw[:, KC]), unfilter(dcw[:, VC]), dhg.reshape(32, 8), head], axis=1
    )
    back_line = jnp.pad(back_line, ((0, 0), (0, 128 - back_line.shape[1])))
    gain_line = jnp.pad(dgain2.reshape(32, 64), ((0, 0), (0, 64)))
    blank = jnp.zeros_like(back_line)
    tiny_back = jnp.stack([back_line, blank, gain_line] + [blank] * 5, axis=1).reshape(4, 4, 2, 8, 128)
    dtok, ra, rt, total = finish(
        stretch_order, dh1, xrows, dm, gain1, grad_a, tiny_back, 6
    )
    ra = ra.astype(f32)
    rgu, rd, ro = rgu.astype(f32), rd.astype(f32), ro.astype(f32)
    rt = rt[:, 0]

    def heads(a):
        return a.swapaxes(0, 1)

    def untaps(a):
        return a.reshape(4, 4, -1).swapaxes(0, 1)

    def narrow(a):
        return a.swapaxes(0, 1).reshape(a.shape[1], -1)[:, :ff]

    return (
        out,
        dtok,
        total[1, :64],
        heads(ra[:, :, 0:128]),
        heads(ra[:, :, 128:256]),
        heads(ra[:, :, 256:512]),
        heads(ra[:, :, 768]),
        heads(ra[:, :, 769]),
        untaps(rt[:, 0:16]),
        untaps(rt[:, 16:32]),
        untaps(rt[:, 32:64]),
        rt[:, 72],
        rt[:, 73],
        total[0, 64:72],
        heads(ra[:, :, 512:768]),
        ro.swapaxes(1, 2),
        total[2, :64],
        narrow(rgu[:, :, :FFP]),
        narrow(rgu[:, :, FFP:]),
        narrow(rd).T,
    )


def solution(mesh):
    torus = Mesh(mesh.devices.reshape(4, 4, 2, 4), ("y", "z", "c", "x"))
    dp, tp = ("y", "z", "c"), "x"
    in_specs = (
        P(dp, None),
        P(dp, None),
        P(),
        P(),
        P(dp),
        P(dp, tp, None),
        P(dp, tp, None),
        P(dp, tp, None),
        P(dp, tp),
        P(dp, tp),
        P(None, tp, dp),
        P(None, tp, dp),
        P(None, tp, dp),
        P(tp),
        P(tp),
        P(dp),
        P(dp, tp, None),
        P(tp, None, dp),
        P(dp),
        P(dp, tp),
        P(dp, tp),
        P(tp, dp),
    )
    out_specs = (
        P(dp, tp),
        P(dp, tp),
        P(dp),
        P(dp, tp, None),
        P(dp, tp, None),
        P(dp, tp, None),
        P(dp, tp),
        P(dp, tp),
        P(None, tp, dp),
        P(None, tp, dp),
        P(None, tp, dp),
        P(tp),
        P(tp),
        P(dp),
        P(dp, tp, None),
        P(tp, None, dp),
        P(dp),
        P(dp, tp),
        P(dp, tp),
        P(tp, dp),
    )
    return jax.shard_map(body, mesh=torus, in_specs=in_specs, out_specs=out_specs, check_vma=False)
```

time: 500 us -> 383 us (0.77)
  Pallas kernels: 376 us -> 299 us
  local copies, waits for them, and re-layouts: 44.5 us -> 20.6 us
  other arithmetic: 26.2 us -> 12.6 us
    pallas_call x12 -> x5, Pallas kernels: 338 us -> 259 us  [the longest x1 62.8 us: fetch(): pl.pallas_call(kernel, out_shape=[shape((4, 4, 2) + pack.shape[1:], bf16)...]
    dot_general x3 -> x0, local copies, waits for them, and re-layouts: 8.51 us -> none  [dot(): lax.dot_general(a, b, (dims, ((), ())), preferred_element_type=f32, preci...]
    concatenate x2 -> x1, other arithmetic: 7.53 us -> 0.08 us  [body(): jnp.concatenate([taps(conv_query), taps(conv_key), taps(conv_value), each...]
    unnamed x90 -> x70, local copies, waits for them, and re-layouts: 10.3 us -> 8.19 us
  transfers between devices with their start and end apart: 1 -> 0, of which waited for: 0 -> 0; matrix products, arithmetic and copies ran while one was open for 4% -> 0% of each run, Pallas kernels for 0% -> 0%
where the time goes in v2:
time: 383 us; the launch traced here: 376 us
  Pallas kernels  299 us (78%)
  matrix products  42 us (11%)
  local copies, waits for them, and re-layouts  20.6 us (5%)
  other arithmetic  12.6 us (3%)
    pallas_call x1, Pallas kernels, fetch(): pl.pallas_call(kernel, out_shape=[shape((4, 4, 2) + pack.shape[1:], bf16)...  62.8 us
    pallas_call x1, Pallas kernels, back_attend(): pl.pallas_call(kernel, out_shape=[shape((128, 512), bf16), shape((SEG, 89...  54.8 us
    pallas_call x1, Pallas kernels, back_middle(): pl.pallas_call(kernel, out_shape=[shape((32, D)), shape((1, D)), shape((4...  50.9 us
    pallas_call x1, Pallas kernels, finish(): pl.pallas_call(kernel, out_shape=[shape((128, 512), bf16), shape((4,) + g...  45.7 us
    pallas_call x1, Pallas kernels, attend(): pl.pallas_call(kernel, out_shape=[shape(pack.shape, bf16), shape((SEG, D)...  44.9 us
    pallas_call x1, Pallas kernels, sum_norm_gather(): pl.pallas_call(kernel, out_shape=[shape((32, D)), shape((4, 4, 32, D), bf...  39.7 us
    dot_general x8, matrix products, dot(): lax.dot_general(a, b, (dims, ((), ())), preferred_element_type=f32, preci...  26.4 us
    unnamed x70, local copies, waits for them, and re-layouts  8.19 us

profile of v2, /device:TPU:1, one launch (start us, length us, event | category | flops | bytes accessed | tf_op | source)
XLA Modules:
  0.0 375.6 jit_solution(6762356535111332640)
XLA Ops:
  6.1 1.0 convert_element_type.93
  7.2 1.1 convert_element_type.94
  10.4 62.8 %shard_map.365 = (bf16[4,4,2,64,1152]{4,3,2,1,0:T(8,128)(2,1)}, f32[4,4,2,8,128]{4,3,2,1,0:T(8,128)}, s32[16]{0:T(128)}, f32[1,2048]{1,0:T(1,128)}, f32[1,2048]{...) custom-call(s32[64]{0:T(128)} %order.5, bf16[2,64,2048]{2,1,0:T(8,128)(2,1)} %bitcast.148, ...), custom_call_target="tpu_custom_call" | custom-call | tf_op jit(solution)/shard_map/pallas_call | solution.py:378
  75.9 6.3 %fusion.2.proj = f32[528,896]{1,0:T(8,128)} fusion(bf16[528,2048]{1,0:T(8,128)(2,1)} %get-tuple-element.63, bf16[2048,1152]{1,0:T(8,128)(2,1)} %bitcast.156), kind=kOutput, calls=%fused_computation.4 | convolution fusion | flops 1937768448 | bytes 7725056 | tf_op jit(solution)/shard_map/dot_general | solution.py:1166
  82.2 44.9 %shard_map.366 = (bf16[4,64,1152]{2,1,0:T(8,128)(2,1)}, bf16[512,2048]{1,0:T(8,128)(2,1)}, bf16[32,2048]{1,0:T(8,128)(2,1)}, bf16[512,512]{1,0:T(8,128)(2,1)}, f...) custom-call(f32[528,896]{1,0:T(8,128)} %fusion.2.proj, ...), custom_call_target="tpu_custom_call" | custom-call | tf_op jit(solution)/shard_map/pallas_call | solution.py:983
  127.1 3.4 convolution_convert_fusion.2
  130.5 39.7 %shard_map.367 = (f32[32,2048]{1,0:T(8,128)}, bf16[4,4,32,2048]{3,2,1,0:T(8,128)(2,1)}, bf16[4,4,2,64,1152]{4,3,2,1,0:T(8,128)(2,1)}) custom-call(bf16[4,4,32,2048]{3,2,1,0:T(8,128)(2,1)} %bitcast.132, bf16[32,2048]{1,0:T(8,128)(2,1)} %get-tuple-element.69.xr, f32[1,2048]{1,0:T(1,128)} %get-tuple-element.70.gain, bf16[4,64,1152]{2,1,0:T(8,128)(2,1)} %get-tuple-element.71.wp), custom_call_target="tpu_custom_call" | custom-call | tf_op jit(solution)/shard_map/pallas_call | solution.py:419
  170.3 4.5 %fusion.8 = f32[512,768]{0,1:T(8,128)S(1)} fusion(bf16[512,2048]{1,0:T(8,128)(2,1)} %bitcast.187, bf16[2048,1152]{1,0:T(8,128)(2,1)} %bitcast.181), kind=kOutput, calls=%fused_computation.12 | convolution fusion | flops 1610612736 | bytes 6815744 | tf_op jit(solution)/shard_map/dot_general | solution.py:1176
  174.9 1.3 multiply_convert_fusion.2
  176.1 2.5 convolution_convert_fusion.5
  178.7 3.5 convolution_convert_fusion.1
  182.2 3.2 convolution_convert_fusion.4
  185.4 2.7 convolution_convert_fusion.3
  188.1 50.9 %shard_map.368 = (f32[32,2048]{1,0:T(8,128)}, f32[1,2048]{1,0:T(1,128)}, bf16[4,4,32,2048]{3,2,1,0:T(8,128)(2,1)}, bf16[4,64,768]{2,1,0:T(8,128)(2,1)}, bf16[4,64,384]{2,1,0:T(8,128)(2,1)}) custom-call(bf16[4,4,32,2048]{3,2,1,0:T(8,128)(2,1)} %bitcast.137, f32[32,2048]{1,0:T(8,128)} %get-tuple-element.74.m, bf16[32,2048]{1,0:T(8,128)(2,1)} %get-tuple-element.75.dy, ...), custom_call_target="tpu_custom_call" | custom-call | tf_op jit(solution)/shard_map/pallas_call | solution.py:467
  239.6 1.4 reduce.17
  241.0 3.5 fusion.14.dn
  244.5 1.7 convolution_convert_fusion.6
  246.3 54.8 %shard_map.369 = (bf16[128,512]{1,0:T(8,128)(2,1)}, bf16[512,896]{1,0:T(8,128)(2,1)}, f32[1,256]{1,0:T(1,128)}, f32[4,512]{1,0:T(4,128)}, f32[2,128]{1,0:T(2,128...) custom-call(f32[512,256]{1,0:T(8,128)} %fusion.14.dn, ...), custom_call_target="tpu_custom_call" | custom-call | tf_op jit(solution)/shard_map/pallas_call | solution.py:1061
  301.2 4.9 %fusion.4 = bf16[512,2048]{1,0:T(8,128)(2,1)} fusion(bf16[512,896]{1,0:T(8,128)(2,1)} %get-tuple-element.92, bf16[2048,1152]{1,0:T(8,128)(2,1)S(1)} %bitcast.161), kind=kOutput, calls=%fused_computation.6 | convolution fusion | flops 1880096768 | bytes 6684672 | tf_op jit(solution)/shard_map/dot_general | solution.py:628
  312.5 4.4 %convolution_convert_fusion = bf16[2048,896]{1,0:T(8,128)(2,1)} fusion(bf16[512,896]{1,0:T(8,128)(2,1)S(1)} %copy-done.21, bf16[528,2048]{1,0:T(8,128)(2,1)S(1)} %copy-done.17), kind=kOutput, calls=%fused_computation | convolution fusion | flops 1880883200 | bytes 6684672 | tf_op jit(solution)/shard_map/dot_general | solution.py:628
  316.9 45.7 %shard_map.370 = (bf16[128,512]{1,0:T(8,128)(2,1)}, bf16[4,64,896]{2,1,0:T(8,128)(2,1)}, f32[4,8,128]{2,1,0:T(8,128)}, f32[8,128]{1,0:T(8,128)}) custom-call(s32[64]{0:T(128)} %order.5, bf16[4,4,32,2048]{3,2,1,0:T(8,128)(2,1)} %bitcast.135, bf16[32,2048]{1,0:T(8,128)(2,1)} %get-tuple-element.69.xr, f32[32,2048]{1,0:T(8,128)} %get-tuple-element.93.dm, ...), custom_call_target="tpu_custom_call" | custom-call | tf_op jit(solution)/shard_map/pallas_call | solution.py:606
  362.7 1.3 slice_bitcast_fusion.7
  363.9 1.3 slice_bitcast_fusion.6
  368.8 1.1 convert_element_type.108
  (152 shorter events, 26.1 us)
Async XLA Ops:
  0.7 7.6 %copy-start.2 = (f32[1376,64]{0,1:T(8,128)S(1)}, f32[1376,64]{0,1:T(8,128)}, u32[]{:S(2)}) copy-start(f32[1376,64]{0,1:T(8,128)} %param.43) | copy-start | bytes 1056772
  7.1 2.2 copy-start.9
  7.2 2.1 copy-start.10
  7.2 2.2 copy-start.3
  8.3 1.2 copy-start.4
  8.3 1.2 copy-start.5
  75.9 6.3 %copy-start.13 = (f32[4,512]{1,0:T(4,128)}, f32[4,512]{1,0:T(4,128)S(1)}, u32[]{:S(2)}) copy-start(f32[4,512]{1,0:T(4,128)S(1)} %constant_dynamic-update-slice_fusion.cw) | copy-start | bytes 24580
  170.3 4.5 %copy-start.16 = (bf16[4,4,2,64,1152]{4,3,2,1,0:T(8,128)(2,1)S(1)}, bf16[4,4,2,64,1152]{4,3,2,1,0:T(8,128)(2,1)}, u32[]{:S(2)}) copy-start(bf16[4,4,2,64,1152]{4,3,2,1,0:T(8,128)(2,1)} %get-tuple-element.72) | copy-start | bytes 14155780
  170.3 4.6 %copy-start.18 = (bf16[512,2048]{1,0:T(8,128)(2,1)S(1)}, bf16[512,2048]{1,0:T(8,128)(2,1)}, u32[]{:S(2)}) copy-start(bf16[512,2048]{1,0:T(8,128)(2,1)} %get-tuple-element.67) | copy-start | bytes 6291460
  176.1 2.6 copy-start.20
  241.0 3.5 copy-start.6
  241.0 3.5 copy-start.19
  244.5 56.6 %slice-start = ((s8[4718592]{0:T(1024)(128)(4,1)}), s8[4194304]{0:T(1024)(128)(4,1)S(1)}, s32[]{:S(2)}) async-start(s8[4718592]{0:T(1024)(128)(4,1)} %bitcast.159), calls=%async_computation | async-start | bytes 8388608
  246.3 54.9 %slice-start.1 = ((s8[4718592]{0:T(1024)(128)(4,1)}), s8[524288]{0:T(1024)(128)(4,1)S(1)}, s32[]{:S(2)}) async-start(s8[4718592]{0:T(1024)(128)(4,1)} %bitcast.159), calls=%async_computation.1 | async-start | bytes 1048576
  301.2 5.0 %copy-start.15 = (f32[1,256]{1,0:T(1,128)S(1)}, f32[1,256]{1,0:T(1,128)}, u32[]{:S(2)}) copy-start(f32[1,256]{1,0:T(1,128)} %get-tuple-element.96) | copy-start | bytes 3076
  301.2 5.7 %copy-start.22 = (f32[2,128]{1,0:T(2,128)S(1)}, f32[2,128]{1,0:T(2,128)}, u32[]{:S(2)}) copy-start(f32[2,128]{1,0:T(2,128)} %get-tuple-element.97) | copy-start | bytes 3076
  301.2 5.8 %copy-start.14 = (f32[4,512]{1,0:T(4,128)S(1)}, f32[4,512]{1,0:T(4,128)}, u32[]{:S(2)}) copy-start(f32[4,512]{1,0:T(4,128)} %get-tuple-element.95) | copy-start | bytes 24580
  301.2 7.6 %copy-start.7 = (bf16[4,64,384]{2,1,0:T(8,128)(2,1)S(1)}, bf16[4,64,384]{2,1,0:T(8,128)(2,1)}, u32[]{:S(2)}) copy-start(bf16[4,64,384]{2,1,0:T(8,128)(2,1)} %get-tuple-element.105) | copy-start | bytes 589828
  306.1 3.5 copy-start.8
  306.1 4.2 %copy-start.1 = (bf16[4,64,768]{2,1,0:T(8,128)(2,1)S(1)}, bf16[4,64,768]{2,1,0:T(8,128)(2,1)}, u32[]{:S(2)}) copy-start(bf16[4,64,768]{2,1,0:T(8,128)(2,1)} %get-tuple-element.104) | copy-start | bytes 1179652
  310.4 1.7 copy-start.17
  310.4 2.1 copy-start.21
  368.8 5.3 %copy-start.11 = (bf16[128,512]{1,0:T(8,128)(2,1)S(1)}, bf16[128,512]{1,0:T(8,128)(2,1)}, u32[]{:S(2)}) copy-start(bf16[128,512]{1,0:T(8,128)(2,1)} %get-tuple-element.211) | copy-start | bytes 393220
  370.0 4.8 %copy-start.12 = (bf16[128,512]{1,0:T(8,128)(2,1)S(1)}, bf16[128,512]{1,0:T(8,128)(2,1)}, u32[]{:S(2)}) copy-start(bf16[128,512]{1,0:T(8,128)(2,1)} %get-tuple-element.212) | copy-start | bytes 393220
  (1 other events, 0.8 us)
